TPU v7x, 32 devices: a whole 2x2x4 slice. The times are simulated.
32 devices in a mesh: dp: 2 (over x), expert: 16 (over z, y, core).
Axes of the slice: x: 2, y: 2, z: 4, core: 2. Of those that a mesh axis runs over, the one named last changes fastest.
Arguments:
- tokens: bfloat16 [4096, 2048], P(('dp', 'expert')), may hold values from -6 to 6
- out_grad: bfloat16 [4096, 2048], P(('dp', 'expert')), may hold values from -6 to 6
- gate_saved: bfloat16 [4096, 6, 1408], P(('dp', 'expert')), may hold values from -6 to 6
- probs: float32 [4096, 6], P(('dp', 'expert')), may hold values from 0.1 to 1
- expert_ids: int32 [4096, 6], P(('dp', 'expert')), may hold values from 0 to 15, all different within a row; in each aligned block of 128 rows (0 to 127, 128 to 255, ...) at most 96 rows name the same one
- w_gate: bfloat16 [16, 2048, 1408], P('expert'), may hold values from -0.125 to 0.125
- w_up: bfloat16 [16, 2048, 1408], P('expert'), may hold values from -0.125 to 0.125
- w_down: bfloat16 [16, 1408, 2048], P('expert'), may hold values from -0.15625 to 0.15625
Outputs:
- input_grad: bfloat16 [4096, 2048], P(('dp', 'expert'))
- grad_gate: bfloat16 [16, 2048, 1408], P('expert', 'dp')
- grad_up: bfloat16 [16, 2048, 1408], P('expert', 'dp')
- grad_down: bfloat16 [16, 1408, 2048], P('expert', 'dp')
Inputs may be any that keep to these rules, and one draw needn't show every extreme that they name: `expert_ids`: each token names 6 different experts. Among the 128 tokens of one aligned block (the tokens of one device) no expert is named more than 96 times, and in some block some expert is named exactly 96 times.
All inputs are finite; a program needn't handle non-finite values.
Results may differ from a plain program's by a relative error of at most 0.013.
Values may be sent and summed in bfloat16 or wider, within the bound.
No kernel may reach another device: no remote copies, remote signals or barrier semaphores. Data moves between devices by JAX's collectives and lax.ppermute only.
A program may use at most 192 MiB of HBM per device.

v0:
```python
import jax
import jax.numpy as jnp
import numpy as np
from jax import lax
from jax.experimental import pallas as pl
from jax.experimental.pallas import tpu as pltpu
from jax.sharding import PartitionSpec as P

grad_scale = 0.0625
f32 = jnp.float32
bf16 = jnp.bfloat16
i32 = jnp.int32
KERNEL_VMEM = 60 * 1024 * 1024
LIGHT = pl.CostEstimate(flops=1000, bytes_accessed=1000, transcendentals=0)


def dot(a, b, dims):
    return lax.dot_general(a, b, (dims, ((), ())), preferred_element_type=f32)


def chunk_widths(width):
    lanes = width // 128
    shares = (3, 7, 11)
    ends = [-(-lanes * x // 11) * 128 for x in shares]
    return [e - s for s, e in zip([0] + ends, ends) if e > s]


def chip_cycle(n_chips):
    cols = n_chips // 4
    if n_chips % 4 or cols < 2:
        return list(range(n_chips))
    walk = [(row, 0) for row in range(4)]
    for step, row in enumerate((3, 2, 1, 0)):
        across = range(1, cols) if step % 2 == 0 else range(cols - 1, 0, -1)
        walk += [(row, col) for col in across]
    return [row * cols + col for row, col in walk]


def put_rows(spots, table, shards, up_mat, down_mat, w, state, cap):
    count = len(shards)
    n_peers = table.shape[0]
    width = shards[0][0].shape[1]
    tok_rows = shards[0][2]

    def body(spots_ref, table_ref, up_ref, down_ref, *refs):
        parts = refs[: 2 * count]
        rows_ref, routed_ref, act_ref, grad_ref = refs[-4:]
        step = pl.program_id(0)
        for i in range(count):

            @pl.when(step == i)
            def _():
                info = table_ref[0]
                place = (
                    lax.broadcasted_iota(i32, (cap, tok_rows), 1).astype(f32) == info[:, 0:1]
                ).astype(bf16)
                rows_ref[...] = jnp.dot(
                    place, parts[2 * i][...], preferred_element_type=f32
                ).astype(bf16)
                picked = jnp.dot(place, parts[2 * i + 1][...], preferred_element_type=f32)
                routed_ref[...] = (info[:, 1:2] * picked).astype(bf16)

        act_ref[...] = jnp.dot(rows_ref[...], up_ref[...], preferred_element_type=f32)
        grad_ref[...] = dot(routed_ref[...], down_ref[...], ((1,), (1,)))

    in_specs = [
        pl.BlockSpec((1, cap, 2), lambda i, spots: (spots[i], 0, 0)),
        pl.BlockSpec((width, w), lambda i, spots: (0, 0)),
        pl.BlockSpec((w, width), lambda i, spots: (0, 0)),
    ]
    operands = [table, up_mat, down_mat]
    for tok, grad, height, tok_at, grad_at in shards:
        in_specs.append(pl.BlockSpec((height, width), lambda i, spots, a=tok_at: (a, 0)))
        in_specs.append(pl.BlockSpec((height, width), lambda i, spots, a=grad_at: (a, 0)))
        operands += [tok, grad]
    aliases = {}
    if state is not None:
        aliases = {1 + len(operands) + j: j for j in range(4)}
        in_specs += [pl.BlockSpec(memory_space=pl.ANY)] * 4
        operands += state
    n_slots = n_peers * cap

    def at(i, spots):
        return (spots[i], 0)

    return pl.pallas_call(
        body,
        out_shape=(
            jax.ShapeDtypeStruct((n_slots, width), bf16),
            jax.ShapeDtypeStruct((n_slots, width), bf16),
            jax.ShapeDtypeStruct((n_slots, w), f32),
            jax.ShapeDtypeStruct((n_slots, w), f32),
        ),
        grid_spec=pltpu.PrefetchScalarGridSpec(
            num_scalar_prefetch=1,
            grid=(count,),
            in_specs=in_specs,
            out_specs=(
                pl.BlockSpec((cap, width), at),
                pl.BlockSpec((cap, width), at),
                pl.BlockSpec((cap, w), at),
                pl.BlockSpec((cap, w), at),
            ),
        ),
        input_output_aliases=aliases,
        compiler_params=pltpu.CompilerParams(vmem_limit_bytes=KERNEL_VMEM),
        cost_estimate=LIGHT,
        name="put_rows",
    )(np.array(spots, np.int32), *operands)


class Ring:
    def __init__(self):
        self.n_peers = lax.axis_size("expert")
        self.n = self.n_peers // 2
        self.far = self.n // 2
        self.names = [self.far]
        for d in range(self.far - 1, 0, -1):
            self.names += [d, -d]
        self.names.append(0)
        cycle = chip_cycle(self.n)
        spot = [cycle.index(c) for c in range(self.n)]
        chips = range(self.n)
        self.fwd = [(2 * cycle[i] + c, 2 * cycle[(i + 1) % self.n] + c) for i in chips for c in (0, 1)]
        self.bwd = [(b, a) for a, b in self.fwd]
        self.swap = [(i, i ^ 1) for i in range(self.n_peers)]
        table = np.zeros((self.n_peers, self.n_peers), np.int32)
        for e in range(self.n_peers):
            for core in (0, 1):
                for j, d in enumerate(self.names):
                    chip = cycle[(spot[e // 2] - d) % self.n]
                    table[e, core * self.n + j] = 2 * chip + (e % 2 if core else 1 - e % 2)
        self.order = jnp.asarray(table)[lax.axis_index("expert")]

    def at(self, distance, other):
        return self.names.index(distance) + (0 if other else self.n)

    def ahead(self, x):
        return lax.ppermute(x, "expert", self.fwd)

    def behind(self, x):
        return lax.ppermute(x, "expert", self.bwd)

    def other_core(self, x):
        return lax.ppermute(x, "expert", self.swap)


def gather_rows(ring, tokens, out_grad, table, cap, up_mat, down_mat, first_width, beside):
    tok_rows = tokens.shape[0]
    own = jnp.concatenate([tokens, out_grad], axis=0)

    def whole(x):
        return (x, x, tok_rows, 0, 1)

    def place(spots, shards, state):
        return put_rows(spots, table, shards, up_mat, down_mat, first_width, state, cap)

    state = None
    ahead, behind = own, own
    pending = ([ring.at(0, False), ring.at(0, True)], [whole(own), whole(ring.other_core(own))])
    for d in range(1, ring.far):
        ahead, behind = ring.ahead(ahead), ring.behind(behind)
        if d >= 2:
            for spots, shards in pending:
                state = place(spots, shards, state)
            pending = []
            ahead, behind, state = lax.optimization_barrier((ahead, behind, state))
            if d == 2:
                ahead, behind, beside = lax.optimization_barrier((ahead, behind, beside))
        else:
            pending = [pending]
        pending.append(
            (
                [ring.at(d, False), ring.at(-d, False), ring.at(d, True), ring.at(-d, True)],
                [whole(x) for x in (ahead, behind, ring.other_core(ahead), ring.other_core(behind))],
            )
        )
    far_tok = ring.ahead(ahead[:tok_rows])
    far_grad = ring.behind(behind[tok_rows:])
    if ring.far == 1:
        pending = [pending]
    for spots, shards in pending:
        state = place(spots, shards, state)
    far_tok, far_grad, state = lax.optimization_barrier((far_tok, far_grad, state))
    theirs_tok, theirs_grad = ring.other_core(far_tok), ring.other_core(far_grad)
    state = place(
        [ring.at(ring.far, False), ring.at(ring.far, True)],
        [(far_tok, far_grad, tok_rows, 0, 0), (theirs_tok, theirs_grad, tok_rows, 0, 0)],
        state,
    )
    return state, (theirs_tok, theirs_grad), beside


def sum_back(ring, theirs, mine, tok_rows, fills):
    handed, ours = {}, {}
    j = 0
    for piece, own in zip(theirs, mine):
        piece = ring.other_core(piece)
        for at in range(0, piece.shape[0], tok_rows):
            handed[ring.names[j]] = piece[at : at + tok_rows]
            ours[ring.names[j]] = own[at : at + tok_rows]
            j += 1

    def plus(d, *others):
        total = ours[d].astype(f32) + handed[d].astype(f32)
        for x in others:
            total = total + x.astype(f32)
        return total.astype(bf16)

    half = tok_rows // 2
    first = plus(ring.far)
    top, low = ring.ahead(first[:half]), ring.behind(first[half:])
    none = jnp.zeros_like(top)
    ahead = jnp.concatenate([top, none], axis=0)
    behind = jnp.concatenate([none, low], axis=0)
    mark, filled = (top, low), []
    for d in range(ring.far - 1, 0, -1):
        ahead, behind = ring.ahead(plus(-d, ahead)), ring.behind(plus(d, behind))
        if len(filled) < len(fills):
            done = fills[len(filled)](mark)
            ahead, behind, done = lax.optimization_barrier((ahead, behind, done))
            filled.append(done)
        mark = (ahead, behind)
    for fill in fills[len(filled) :]:
        filled.append(fill(mark))
    return plus(0, ahead, behind), filled


def blocks_per_step(n_blocks, cap):
    return max(b for b in range(1, n_blocks + 1) if n_blocks % b == 0 and b * cap <= 768)


def chunk_grads(order, cols, rows, routed, gate, up_mat, down_mat, start, piece, ready):
    n_slots, width = rows.shape
    n_peers, cap, w = gate.shape
    n = blocks_per_step(n_peers, cap)
    r = n * cap
    n_rows, n_cols = n_slots // r, cols.shape[0]
    n_in = 4 if ready is None else 2

    def body(order_ref, cols_ref, *refs):
        ins, col_ref, gate_refs = refs[:n_in], refs[n_in], refs[n_in + 1 : n_in + 1 + n]
        hidden_ref, both_ref, part_ref, held = refs[n_in + 1 + n :]
        step = pl.program_id(0)

        @pl.when(step < n_rows)
        def _():
            if ready is None:
                up_all = jnp.dot(ins[0][...], ins[2][...], preferred_element_type=f32)
                grad_all = dot(ins[1][...], ins[3][...], ((1,), (1,)))
            else:
                up_all, grad_all = ins
            for b in range(n):
                at = slice(b * cap, (b + 1) * cap)
                up_act, hidden_grad = up_all[at, :], grad_all[at, :]
                gate_val = gate_refs[b][0].astype(f32)
                gate_sig = jax.nn.sigmoid(gate_val)
                gate_act = gate_val * gate_sig
                hidden_ref[at, :] = (gate_act * up_act).astype(bf16)
                both_ref[at, w:] = (hidden_grad * gate_act).astype(bf16)
                both_ref[at, :w] = (
                    hidden_grad * up_act * gate_sig * (1.0 + gate_val * (1.0 - gate_sig))
                ).astype(bf16)
            held[pl.ds(pl.multiple_of(step * r, r), r), :] = both_ref[...]

        @pl.when(step >= n_rows)
        def _():
            part_ref[...] = dot(col_ref[...], held[...], ((0,), (0,))).astype(bf16)

    def row(i):
        return jnp.minimum(i, n_rows - 1)

    def col(i):
        return jnp.maximum(i - n_rows, 0)

    def row_blocks(x):
        return pl.BlockSpec((r, x.shape[1]), lambda i, order, cols: (row(i), 0))

    if ready is None:
        operands = [rows, routed, up_mat, down_mat]
        in_specs = [
            row_blocks(rows),
            row_blocks(routed),
            pl.BlockSpec((pl.Element(width), pl.Element(w)), lambda i, order, cols: (0, start)),
            pl.BlockSpec((pl.Element(w), pl.Element(width)), lambda i, order, cols: (start, 0)),
        ]
    else:
        operands = list(ready)
        in_specs = [row_blocks(x) for x in ready]
    return pl.pallas_call(
        body,
        out_shape=(
            jax.ShapeDtypeStruct((n_slots, w), bf16),
            jax.ShapeDtypeStruct((n_slots, 2 * w), bf16),
            jax.ShapeDtypeStruct((n_cols * piece, 2 * w), bf16),
        ),
        grid_spec=pltpu.PrefetchScalarGridSpec(
            num_scalar_prefetch=2,
            grid=(n_rows + n_cols,),
            in_specs=in_specs
            + [pl.BlockSpec((n_slots, piece), lambda i, order, cols: (0, cols[col(i)]))]
            + [
                pl.BlockSpec((1, cap, w), lambda i, order, cols, b=b: (order[n * row(i) + b], 0, 0))
                for b in range(n)
            ],
            out_specs=(
                pl.BlockSpec((r, w), lambda i, order, cols: (row(i), 0)),
                pl.BlockSpec((r, 2 * w), lambda i, order, cols: (row(i), 0)),
                pl.BlockSpec((piece, 2 * w), lambda i, order, cols: (col(i), 0)),
            ),
            scratch_shapes=[pltpu.VMEM((n_slots, 2 * w), bf16)],
        ),
        compiler_params=pltpu.CompilerParams(vmem_limit_bytes=KERNEL_VMEM),
        cost_estimate=LIGHT,
        name="chunk_grads",
    )(order, cols, *operands, rows, *[gate] * n)


def own_half(cols, rows, both, piece):
    n_slots = rows.shape[0]
    w = both.shape[1]

    def body(cols_ref, rows_ref, both_ref, own_ref):
        own_ref[...] = dot(rows_ref[...], both_ref[...], ((0,), (0,))).astype(bf16)

    return pl.pallas_call(
        body,
        out_shape=jax.ShapeDtypeStruct((piece, w), bf16),
        grid_spec=pltpu.PrefetchScalarGridSpec(
            num_scalar_prefetch=1,
            grid=(1,),
            in_specs=[
                pl.BlockSpec((n_slots, piece), lambda i, cols: (0, cols[0])),
                pl.BlockSpec((n_slots, w), lambda i, cols: (0, 0)),
            ],
            out_specs=pl.BlockSpec((piece, w), lambda i, cols: (0, 0)),
        ),
        compiler_params=pltpu.CompilerParams(vmem_limit_bytes=KERNEL_VMEM),
        cost_estimate=LIGHT,
        name="own_half",
    )(cols, rows, both)


def down_rows(routed, hidden, start, total, hidden_width):
    n_slots, width = routed.shape
    w = hidden.shape[1]
    span = min(1024, width)

    def body(routed_ref, hidden_ref, *refs):
        down_ref, turned = refs[-2:]

        @pl.when(pl.program_id(0) == 0)
        def _():
            turned[...] = hidden_ref[...].T

        down_ref[...] = jnp.dot(turned[...], routed_ref[...], preferred_element_type=f32).astype(bf16)

    aliased = [] if total is None else [total]
    return pl.pallas_call(
        body,
        out_shape=jax.ShapeDtypeStruct((hidden_width, width), bf16),
        grid=(width // span,),
        in_specs=[
            pl.BlockSpec((n_slots, span), lambda i: (0, i)),
            pl.BlockSpec((n_slots, w), lambda i: (0, 0)),
        ]
        + [pl.BlockSpec(memory_space=pl.ANY) for _ in aliased],
        out_specs=pl.BlockSpec((pl.Element(w), pl.Element(span)), lambda i: (start, i * span)),
        scratch_shapes=[pltpu.VMEM((w, n_slots), bf16)],
        input_output_aliases={2: 0} if aliased else {},
        compiler_params=pltpu.CompilerParams(vmem_limit_bytes=KERNEL_VMEM),
        cost_estimate=LIGHT,
        name="down_rows",
    )(routed, hidden, *aliased)


def join_halves(own, arrived, start, totals, hidden_width):
    piece, both_width = own.shape
    w = both_width // 2
    r = min(256, piece)
    n_in = 1 + len(arrived)

    def body(*refs):
        gate_ref, up_ref = refs[-2:]
        for at, out_ref in ((slice(0, w), gate_ref), (slice(w, 2 * w), up_ref)):
            total = refs[0][:, at].astype(f32)
            for x in refs[1:n_in]:
                total = total + x[:, at].astype(f32)
            out_ref[...] = (grad_scale * total).astype(bf16)

    aliased = [] if totals is None else list(totals)
    shape = jax.ShapeDtypeStruct((piece, hidden_width), bf16)
    out_spec = pl.BlockSpec((pl.Element(r), pl.Element(w)), lambda i: (i * r, start))
    return pl.pallas_call(
        body,
        out_shape=(shape, shape),
        grid=(piece // r,),
        in_specs=[pl.BlockSpec((r, both_width), lambda i: (i, 0))] * n_in
        + [pl.BlockSpec(memory_space=pl.ANY) for _ in aliased],
        out_specs=(out_spec, out_spec),
        input_output_aliases={n_in: 0, n_in + 1: 1} if aliased else {},
        compiler_params=pltpu.CompilerParams(vmem_limit_bytes=KERNEL_VMEM),
        cost_estimate=LIGHT,
        name="join_halves",
    )(own, *arrived, *aliased)


def spread_back(parts, starts, gate_mat, up_mat, table, tok_rows, first, heights):
    n_peers, _, cap = table.shape
    half = n_peers // 2
    width, hidden_width = gate_mat.shape
    cols = min(512, width)
    rows = half * cap
    shift = 0 if first else 1
    owner = [(i, b) for i, height in enumerate(heights) for b in range(height)]

    def body(*refs):
        part_refs = refs[: len(parts)]
        gate_ref, up_ref, table_ref = refs[len(parts) : len(parts) + 3]
        out_refs = refs[len(parts) + 3 :]
        total = jnp.zeros((rows, cols), f32)
        for start, part_ref in zip(starts, part_refs):
            w = part_ref.shape[1] // 2
            total += dot(part_ref[:, :w], gate_ref[:, start : start + w], ((1,), (1,)))
            total += dot(part_ref[:, w:], up_ref[:, start : start + w], ((1,), (1,)))
        terms = total.astype(bf16)
        for j, (i, b) in enumerate(owner):
            tok = table_ref[j, 0:1, :]
            place = (lax.broadcasted_iota(i32, (tok_rows, cap), 0).astype(f32) == tok).astype(bf16)
            spread = jnp.dot(place, terms[j * cap : (j + 1) * cap], preferred_element_type=f32)
            out_refs[i][b * tok_rows : (b + 1) * tok_rows, :] = spread.astype(bf16)

    return pl.pallas_call(
        body,
        out_shape=[jax.ShapeDtypeStruct((h * tok_rows, width), bf16) for h in heights],
        grid=(width // cols,),
        in_specs=[pl.BlockSpec((rows, x.shape[1]), lambda j: (shift, 0)) for x in parts]
        + [
            pl.BlockSpec((cols, hidden_width), lambda j: (j, 0)),
            pl.BlockSpec((cols, hidden_width), lambda j: (j, 0)),
            pl.BlockSpec((half, 2, cap), lambda j: (shift, 0, 0)),
        ],
        out_specs=[pl.BlockSpec((h * tok_rows, cols), lambda j: (0, j)) for h in heights],
        compiler_params=pltpu.CompilerParams(vmem_limit_bytes=KERNEL_VMEM),
        cost_estimate=LIGHT,
        name="spread_back",
    )(*parts, gate_mat, up_mat, table)


def local(tokens, out_grad, gate_saved, probs, expert_ids, w_gate, w_up, w_down):
    n_peers = lax.axis_size("expert")
    n_dp = lax.axis_size("dp")
    group = lax.axis_index("dp")
    tok_rows, model_width = tokens.shape
    top_k = expert_ids.shape[1]
    hidden_width = w_up.shape[2]
    cap = min(tok_rows, 2 * tok_rows * top_k // n_peers)
    n_routes = tok_rows * top_k
    n_slots = n_peers * cap
    gate_mat, up_mat, down_mat = w_gate[0], w_up[0], w_down[0]

    experts = jnp.arange(n_peers, dtype=i32)
    hit = expert_ids[:, :, None] == experts[None, None, :]
    named = jnp.any(hit, axis=1)
    weight = jnp.sum(jnp.where(hit, probs[:, :, None], 0.0), axis=1)
    rank = jnp.cumsum(named.astype(i32), axis=0) - 1
    slots = jnp.arange(cap, dtype=i32)
    in_slot = named[:, :, None] & (rank[:, :, None] == slots[None, None, :])
    tok_of = jnp.sum(
        jnp.where(in_slot, jnp.arange(1, tok_rows + 1, dtype=f32)[:, None, None], 0.0), axis=0
    ) - 1.0
    choice = jnp.sum(jnp.where(hit, jnp.arange(top_k, dtype=f32)[None, :, None], 0.0), axis=1)
    choice_of = jnp.sum(jnp.where(in_slot, choice[:, :, None], 0.0), axis=0)
    weight_of = jnp.sum(jnp.where(in_slot, weight[:, :, None], 0.0), axis=0)
    table = lax.all_to_all(
        jnp.concatenate([tok_of, weight_of], axis=1),
        "expert",
        split_axis=0,
        concat_axis=0,
        tiled=True,
    )
    ring = Ring()
    table = table.reshape(n_peers, 2, cap)[ring.order]
    widths = chunk_widths(hidden_width)
    starts = [sum(widths[:i]) for i in range(len(widths))]
    route_gates = jnp.transpose(gate_saved, (1, 0, 2)).reshape(n_routes, hidden_width)
    route_of = (tok_of + tok_rows * choice_of).astype(i32).reshape(n_slots, 1)
    pick = (route_of == jnp.arange(n_routes, dtype=i32)[None, :]).astype(bf16)
    send_gate = [
        dot(pick, route_gates[:, s : s + w], ((1,), (0,))).astype(bf16).reshape(n_peers, cap, w)
        for s, w in zip(starts, widths)
    ]
    (rows_in, routed, up_first, grad_first), mark, send_gate[1:] = gather_rows(
        ring,
        tokens,
        out_grad,
        table.transpose(0, 2, 1),
        cap,
        up_mat,
        down_mat,
        widths[0],
        send_gate[1:],
    )

    def send_chunk(i, mark):
        part = send_gate[i]
        if mark is not None:
            part, _ = lax.optimization_barrier((part, mark))
        return lax.all_to_all(part, "expert", split_axis=0, concat_axis=0, tiled=True)

    recv_gate = [send_chunk(i, mark) for i, mark in zip(range(len(widths)), (None, mark))]

    piece = model_width // n_dp
    shifts = [[(i, (i + d) % n_dp) for i in range(n_dp)] for d in range(n_dp)]

    peer_cols = lax.rem(group + jnp.arange(1, n_dp, dtype=i32), n_dp)
    own_cols = group.reshape(1).astype(i32)
    both_parts, arrivals, own_parts = [], [], []
    sum_down = None
    rows_now, routed_now = rows_in, routed
    for c, w in enumerate(widths):
        hidden, both, sent = chunk_grads(
            ring.order,
            peer_cols,
            rows_now,
            routed_now,
            recv_gate[c],
            up_mat,
            down_mat,
            starts[c],
            piece,
            (up_first, grad_first) if c == 0 else None,
        )
        both_parts.append(both)
        arrivals.append(
            [
                lax.ppermute(sent[(d - 1) * piece : d * piece], "dp", shifts[d])
                for d in range(1, n_dp)
            ]
        )
        if c + 1 < len(widths):
            own = own_half(own_cols, rows_now, both, piece)
            sum_down = down_rows(routed_now, hidden, starts[c], sum_down, hidden_width)
            if c + 2 < len(widths):
                recv_gate.append(send_chunk(c + 2, own))
            if c >= 1:
                rows_now, arrivals[c - 1] = lax.optimization_barrier((rows_now, arrivals[c - 1]))
            rows_now, routed_now, own, sum_down = lax.optimization_barrier(
                (rows_now, routed_now, own, sum_down)
            )
            own_parts.append(own)

    heights = [1] + [2] * (ring.far - 1) + [1]
    theirs = spread_back(both_parts, starts, gate_mat, up_mat, table, tok_rows, True, heights)
    hidden, _ = lax.optimization_barrier((hidden, theirs))
    sum_down = down_rows(routed_now, hidden, starts[-1], sum_down, hidden_width)
    low = hidden_width // n_dp
    sent = [
        lax.dynamic_slice_in_dim(sum_down, lax.rem(group + d, n_dp) * low, low, 0)
        for d in range(1, n_dp)
    ]
    last, arrivals[:-1], sent = lax.optimization_barrier((both, arrivals[:-1], sent))
    arrived = [lax.ppermute(part, "dp", shifts[d]) for d, part in enumerate(sent, 1)]
    mine = spread_back(
        both_parts[:-1] + [last], starts, gate_mat, up_mat, table, tok_rows, False, heights
    )
    mine, arrivals[-1] = lax.optimization_barrier((mine, arrivals[-1]))

    def last_half(mark):
        held, _ = lax.optimization_barrier((both, mark))
        return own_half(own_cols, rows_now, held, piece), arrivals[-1]

    def join_first(mark):
        parts, _ = lax.optimization_barrier((own_parts, mark))
        joined = None
        for c, part in enumerate(parts):
            joined = join_halves(part, arrivals[c], starts[c], joined, hidden_width)
        return joined

    input_grad, ((own, arrivals[-1]), totals) = sum_back(
        ring, theirs, mine, tok_rows, [last_half, join_first]
    )
    arrived, _ = lax.optimization_barrier((arrived, input_grad))
    grad_gate, grad_up = join_halves(own, arrivals[-1], starts[-1], totals, hidden_width)
    down = lax.dynamic_slice_in_dim(sum_down, group * low, low, 0).astype(f32)
    for part in arrived:
        down = down + part.astype(f32)
    grad_down = (grad_scale * down).astype(bf16)[None]
    return (input_grad, grad_gate[None], grad_up[None], grad_down)


def solution(mesh):
    return jax.shard_map(
        local,
        mesh=mesh,
        in_specs=(
            P(("dp", "expert"), None),
            P(("dp", "expert"), None),
            P(("dp", "expert"), None, None),
            P(("dp", "expert"), None),
            P(("dp", "expert"), None),
            P("expert", None, None),
            P("expert", None, None),
            P("expert", None, None),
        ),
        out_specs=(
            P(("dp", "expert"), None),
            P("expert", "dp", None),
            P("expert", "dp", None),
            P("expert", "dp", None),
        ),
        check_vma=False,
    )
```

profile of v0, /device:TPU:0, one launch (start us, length us, event | category | flops | bytes accessed | tf_op | source)
XLA Modules:
  0.0 433.2 jit_solution(1522768295052217697)
XLA Ops:
  8.6 20.4 %collective-permute-done.refs_0_.refs_1_ = bf16[256,2048]{1,0:T(8,128)(2,1)S(1)} collective-permute-done((bf16[256,2048]{1,0:T(8,128)(2,1)S(1)}, bf16[256,2048]{1,0:T(8,128)(2,1)S(1)}, u32[]{:S(2)}, u32[]{:S(2)}) %collective-permute-start) | collective-permute-done | bytes 1048608 | tf_op jit(solution)/shard_map/ppermute | solution.py:139
  46.4 12.1 %all-to-all-done = f32[16,1,192]{2,1,0:T(1,128)S(1)} async-done(((f32[16,1,192]{2,1,0:T(1,128)}), f32[16,1,192]{2,1,0:T(1,128)S(1)}, u32[]{:S(2)}, u32[]{:S(2)}) %all-to-all-start) | async-done | bytes 12320 | tf_op jit(solution)/shard_map/all_to_all | solution.py:475
  67.1 10.0 %put_rows.6 = (bf16[1536,2048]{1,0:T(8,128)(2,1)}, bf16[1536,2048]{1,0:T(8,128)(2,1)}, f32[1536,384]{1,0:T(8,128)}, f32[1536,384]{1,0:T(8,128)}) custom-call(s32[4]{0:T(128)} %constant.67.clone.spots_ref, f32[16,96,2]{2,1,0:T(8,128)} %copy.61.table_ref, ...), custom_call_target="tpu_custom_call", output_to_operand_aliasing={{0}: (12, {}), {1}: (13, {}), {2}: (14, {}), {3}: (15, {})} | custom-call | flops 1000 | bytes 1000 | tf_op jit(solution)/shard_map/put_rows/pallas_call | solution.py:86
  87.4 10.0 %put_rows.7 = (bf16[1536,2048]{1,0:T(8,128)(2,1)}, bf16[1536,2048]{1,0:T(8,128)(2,1)}, f32[1536,384]{1,0:T(8,128)}, f32[1536,384]{1,0:T(8,128)}) custom-call(s32[4]{0:T(128)} %constant.68.clone.spots_ref, f32[16,96,2]{2,1,0:T(8,128)} %copy.61.table_ref, ...), custom_call_target="tpu_custom_call", output_to_operand_aliasing={{0}: (12, {}), {1}: (13, {}), {2}: (14, {}), {3}: (15, {})} | custom-call | flops 1000 | bytes 1000 | tf_op jit(solution)/shard_map/put_rows/pallas_call | solution.py:86
  97.4 7.0 %collective-permute-done.7.refs_0_.refs_1_ = bf16[256,2048]{1,0:T(8,128)(2,1)S(1)} collective-permute-done((bf16[256,2048]{1,0:T(8,128)(2,1)}, bf16[256,2048]{1,0:T(8,128)(2,1)S(1)}, u32[]{:S(2)}, u32[]{:S(2)}) %collective-permute-start.7) | collective-permute-done | bytes 1048608 | tf_op jit(solution)/shard_map/ppermute | solution.py:139
  114.4 10.0 %put_rows.8 = (bf16[1536,2048]{1,0:T(8,128)(2,1)}, bf16[1536,2048]{1,0:T(8,128)(2,1)}, f32[1536,384]{1,0:T(8,128)}, f32[1536,384]{1,0:T(8,128)}) custom-call(s32[4]{0:T(128)} %constant.69.clone.spots_ref, f32[16,96,2]{2,1,0:T(8,128)} %copy.61.table_ref, ...), custom_call_target="tpu_custom_call", output_to_operand_aliasing={{0}: (12, {}), {1}: (13, {}), {2}: (14, {}), {3}: (15, {})} | custom-call | flops 1000 | bytes 1000 | tf_op jit(solution)/shard_map/put_rows/pallas_call | solution.py:86
  124.3 7.3 %collective-permute-done.11.refs_0_ = bf16[128,2048]{1,0:T(8,128)(2,1)S(1)} collective-permute-done((bf16[128,2048]{1,0:T(8,128)(2,1)}, bf16[128,2048]{1,0:T(8,128)(2,1)S(1)}, u32[]{:S(2)}, u32[]{:S(2)}) %collective-permute-start.11) | collective-permute-done | bytes 524320 | tf_op jit(solution)/shard_map/ppermute | solution.py:139
  137.1 10.1 %all-to-all-start.2 = ((bf16[16,96,512]{2,1,0:T(8,128)(2,1)}), bf16[16,96,512]{2,1,0:T(8,128)(2,1)S(1)}, u32[]{:S(2)}, u32[]{:S(2)}) async-start(bf16[16,96,512]{2,1,0:T(8,128)(2,1)} %bitcast.44), calls=%async_computation.2 | async-start | bytes 3145728 | tf_op jit(solution)/shard_map/all_to_all | solution.py:509
  148.4 6.6 %put_rows.9 = (bf16[1536,2048]{1,0:T(8,128)(2,1)}, bf16[1536,2048]{1,0:T(8,128)(2,1)}, f32[1536,384]{1,0:T(8,128)}, f32[1536,384]{1,0:T(8,128)}) custom-call(s32[2]{0:T(128)} %constant.70.clone.spots_ref, f32[16,96,2]{2,1,0:T(8,128)} %copy.61.table_ref, ...), custom_call_target="tpu_custom_call", output_to_operand_aliasing={{0}: (8, {}), {1}: (9, {}), {2}: (10, {}), {3}: (11, {})} | custom-call | flops 1000 | bytes 1000 | tf_op jit(solution)/shard_map/put_rows/pallas_call | solution.py:86
  155.0 10.2 %chunk_grads.3 = (bf16[1536,384]{1,0:T(8,128)(2,1)}, bf16[1536,768]{1,0:T(8,128)(2,1)}, bf16[1024,768]{1,0:T(8,128)(2,1)}) custom-call(s32[16]{0:T(128)} %fusion.16.order_ref, s32[1]{0:T(128)S(6)} %rem.31.cols_ref, f32[1536,384]{1,0:T(8,128)} %get-tuple-element.142.refs_0_, f32[1536,384]{1,0:T(8,128)} %get-tuple-element.143.refs_1_, ...), custom_call_target="tpu_custom_call" | custom-call | flops 1000 | bytes 1000 | tf_op jit(solution)/shard_map/chunk_grads/pallas_call | solution.py:290
  171.7 7.5 %all-to-all-done.2.refs_5_.refs_6_.refs_7_.refs_8_.refs_9_.refs_10_.refs_11_.refs_12_ = bf16[16,96,512]{2,1,0:T(8,128)(2,1)S(1)} async-done(((bf16[16,96,512]{2,1,0:T(8,128)(2,1)}), bf16[16,96,512]{2,1,0:T(8,128)(2,1)S(1)}, u32[]{:S(2)}, u32[]{:S(2)}) %all-to-all-start.2) | async-done | bytes 1572896 | tf_op jit(solution)/shard_map/all_to_all | solution.py:509
  179.2 9.3 %all-to-all-start.3 = ((bf16[16,96,512]{2,1,0:T(8,128)(2,1)}), bf16[16,96,512]{2,1,0:T(8,128)(2,1)S(1)}, u32[]{:S(2)}, u32[]{:S(2)}) async-start(bf16[16,96,512]{2,1,0:T(8,128)(2,1)} %bitcast.43), calls=%async_computation.3 | async-start | bytes 3145728 | tf_op jit(solution)/shard_map/all_to_all | solution.py:509
  196.3 29.4 %collective-permute-done.17.refs_1_ = bf16[1024,768]{1,0:T(8,128)(2,1)} collective-permute-done((bf16[1024,768]{1,0:T(8,128)(2,1)}, bf16[1024,768]{1,0:T(8,128)(2,1)}, u32[]{:S(2)}, u32[]{:S(2)}) %collective-permute-start.17) | collective-permute-done | bytes 1572896 | tf_op jit(solution)/shard_map/ppermute | solution.py:537
  225.7 19.9 %chunk_grads.4 = (bf16[1536,512]{1,0:T(8,128)(2,1)}, bf16[1536,1024]{1,0:T(8,128)(2,1)}, bf16[1024,1024]{1,0:T(8,128)(2,1)}) custom-call(s32[16]{0:T(128)} %fusion.16.order_ref, s32[1]{0:T(128)S(6)} %rem.31.cols_ref, bf16[1536,2048]{1,0:T(8,128)(2,1)} %get-tuple-element.157.refs_2_.rows_ref.refs_0_.refs_4_, ...), custom_call_target="tpu_custom_call" | custom-call | flops 1000 | bytes 1000 | tf_op jit(solution)/shard_map/chunk_grads/pallas_call | solution.py:290
  245.6 7.6 %own_half.4.refs_0_ = bf16[1024,1024]{1,0:T(8,128)(2,1)} custom-call(s32[1]{0:T(128)} %bitcast.1.cols_ref, bf16[1536,2048]{1,0:T(8,128)(2,1)} %get-tuple-element.157.refs_2_.rows_ref.refs_0_.refs_4_, bf16[1536,1024]{1,0:T(8,128)(2,1)} %get-tuple-element.152.both_ref.refs_1_), custom_call_target="tpu_custom_call" | custom-call | flops 1000 | bytes 1000 | tf_op jit(solution)/shard_map/own_half/pallas_call | solution.py:326
  253.2 7.5 %down_rows.4.refs_0_ = bf16[1408,2048]{1,0:T(8,128)(2,1)} custom-call(bf16[1536,2048]{1,0:T(8,128)(2,1)} %get-tuple-element.158.routed_ref.refs_1_, bf16[1536,512]{1,0:T(8,128)(2,1)} %get-tuple-element.155.hidden_ref, bf16[1408,2048]{1,0:T(8,128)(2,1)} %down_rows.3.refs_0_), custom_call_target="tpu_custom_call", output_to_operand_aliasing={{}: (2, {})} | custom-call | flops 1000 | bytes 1000 | tf_op jit(solution)/shard_map/down_rows/pallas_call | solution.py:359
  263.3 20.0 %chunk_grads.5 = (bf16[1536,512]{1,0:T(8,128)(2,1)}, bf16[1536,1024]{1,0:T(8,128)(2,1)}, bf16[1024,1024]{1,0:T(8,128)(2,1)}) custom-call(s32[16]{0:T(128)} %fusion.16.order_ref, s32[1]{0:T(128)S(6)} %rem.31.cols_ref, bf16[1536,2048]{1,0:T(8,128)(2,1)} %get-tuple-element.157.refs_2_.rows_ref.refs_0_.refs_4_, ...), custom_call_target="tpu_custom_call" | custom-call | flops 1000 | bytes 1000 | tf_op jit(solution)/shard_map/chunk_grads/pallas_call | solution.py:290
  284.0 15.6 %spread_back.2 = (bf16[128,2048]{1,0:T(8,128)(2,1)}, bf16[256,2048]{1,0:T(8,128)(2,1)}, bf16[256,2048]{1,0:T(8,128)(2,1)}, bf16[256,2048]{1,0:T(8,128)(2,1)}, bf16[128,2048]{1,0:T(8,128)(2,1)}) custom-call(bf16[1536,768]{1,0:T(8,128)(2,1)} %get-tuple-element.145.both_ref.refs_0_, bf16[1536,1024]{1,0:T(8,128)(2,1)} %get-tuple-element.152.both_ref.refs_1_, ...), custom_call_target="tpu_custom_call" | custom-call | flops 1000 | bytes 1000 | tf_op jit(solution)/shard_map/spread_back/pallas_call | solution.py:433
  300.2 7.4 %down_rows.5 = bf16[1408,2048]{1,0:T(8,128)(2,1)} custom-call(bf16[1536,2048]{1,0:T(8,128)(2,1)} %get-tuple-element.158.routed_ref.refs_1_, bf16[1536,512]{1,0:T(8,128)(2,1)} %get-tuple-element.170.hidden_ref, bf16[1408,2048]{1,0:T(8,128)(2,1)} %down_rows.4.refs_0_), custom_call_target="tpu_custom_call", output_to_operand_aliasing={{}: (2, {})} | custom-call | flops 1000 | bytes 1000 | tf_op jit(solution)/shard_map/down_rows/pallas_call | solution.py:359
  309.6 15.7 %spread_back.3 = (bf16[128,2048]{1,0:T(8,128)(2,1)}, bf16[256,2048]{1,0:T(8,128)(2,1)}, bf16[256,2048]{1,0:T(8,128)(2,1)}, bf16[256,2048]{1,0:T(8,128)(2,1)}, bf16[128,2048]{1,0:T(8,128)(2,1)}) custom-call(bf16[1536,768]{1,0:T(8,128)(2,1)} %get-tuple-element.145.both_ref.refs_0_, bf16[1536,1024]{1,0:T(8,128)(2,1)} %get-tuple-element.152.both_ref.refs_1_, ...), custom_call_target="tpu_custom_call" | custom-call | flops 1000 | bytes 1000 | tf_op jit(solution)/shard_map/spread_back/pallas_call | solution.py:433
  325.3 27.8 %collective-permute-done.19.refs_1_ = bf16[1024,1024]{1,0:T(8,128)(2,1)} collective-permute-done((bf16[1024,1024]{1,0:T(8,128)(2,1)}, bf16[1024,1024]{1,0:T(8,128)(2,1)}, u32[]{:S(2)}, u32[]{:S(2)}) %collective-permute-start.19) | collective-permute-done | bytes 2097184 | tf_op jit(solution)/shard_map/ppermute | solution.py:537
  367.4 7.6 %own_half.5.refs_0_ = bf16[1024,1024]{1,0:T(8,128)(2,1)} custom-call(s32[1]{0:T(128)} %bitcast.1.cols_ref, bf16[1536,2048]{1,0:T(8,128)(2,1)} %get-tuple-element.157.refs_2_.rows_ref.refs_0_.refs_4_, bf16[1536,1024]{1,0:T(8,128)(2,1)} %get-tuple-element.184.refs_2_.both_ref), custom_call_target="tpu_custom_call" | custom-call | flops 1000 | bytes 1000 | tf_op jit(solution)/shard_map/own_half/pallas_call | solution.py:326
  403.5 6.6 %collective-permute-done.32 = bf16[128,2048]{1,0:T(8,128)(2,1)} collective-permute-done((bf16[128,2048]{1,0:T(8,128)(2,1)}, bf16[128,2048]{1,0:T(8,128)(2,1)}, u32[]{:S(2)}, u32[]{:S(2)}) %collective-permute-start.32) | collective-permute-done | bytes 524320 | tf_op jit(solution)/shard_map/ppermute | solution.py:142
  413.4 13.6 %collective-permute-done.33 = bf16[704,2048]{1,0:T(8,128)(2,1)} collective-permute-done((bf16[704,2048]{1,0:T(8,128)(2,1)S(1)}, bf16[704,2048]{1,0:T(8,128)(2,1)}, u32[]{:S(2)}, u32[]{:S(2)}) %collective-permute-start.33) | collective-permute-done | bytes 2883616 | tf_op jit(solution)/shard_map/ppermute | solution.py:563
  (134 shorter events, 132.7 us)
Async XLA Ops:
  2.8 26.2 %collective-permute-start = (bf16[256,2048]{1,0:T(8,128)(2,1)S(1)}, bf16[256,2048]{1,0:T(8,128)(2,1)S(1)}, u32[]{:S(2)}, u32[]{:S(2)}) collective-permute-start(bf16[256,2048]{1,0:T(8,128)(2,1)S(1)} %constant_dynamic-update-slice_fusion.refs_0_.refs_1_), channel_id=1, source_target_pairs={{0,4},{1,5},{4,8},{5,9},{8,12},{9,13},{12,14},{13,15},{14,10},{15,... | collective-permute-start | bytes 3145736 | tf_op jit(solution)/shard_map/ppermute | solution.py:139
  5.9 24.9 %collective-permute-start.2 = (bf16[256,2048]{1,0:T(8,128)(2,1)S(1)}, bf16[256,2048]{1,0:T(8,128)(2,1)S(1)}, u32[]{:S(2)}, u32[]{:S(2)}) collective-permute-start(bf16[256,2048]{1,0:T(8,128)(2,1)S(1)} %constant_dynamic-update-slice_fusion.refs_0_.refs_1_), channel_id=1, source_target_pairs={{4,0},{5,1},{8,4},{9,5},{12,8},{13,9},{14,12},{15,13},{10,14},{11,... | collective-permute-start | bytes 3145736 | tf_op jit(solution)/shard_map/ppermute | solution.py:142
  5.9 54.6 %collective-permute-start.6 = (bf16[256,2048]{1,0:T(8,128)(2,1)S(1)}, bf16[256,2048]{1,0:T(8,128)(2,1)}, u32[]{:S(2)}, u32[]{:S(2)}) collective-permute-start(bf16[256,2048]{1,0:T(8,128)(2,1)S(1)} %constant_dynamic-update-slice_fusion.refs_0_.refs_1_), channel_id=1, source_target_pairs={{0,1},{1,0},{2,3},{3,2},{4,5},{5,4},{6,7},{7,6},{8,9},{9,8},{10,11... | collective-permute-start | bytes 3145736 | tf_op jit(solution)/shard_map/ppermute | solution.py:145
  29.0 48.1 %collective-permute-start.1 = (bf16[256,2048]{1,0:T(8,128)(2,1)S(1)}, bf16[256,2048]{1,0:T(8,128)(2,1)}, u32[]{:S(2)}, u32[]{:S(2)}) collective-permute-start(bf16[256,2048]{1,0:T(8,128)(2,1)S(1)} %collective-permute-done.refs_0_.refs_1_), channel_id=1, source_target_pairs={{0,4},{1,5},{4,8},{5,9},{8,12},{9,13},{12,14},{13,15},{14,10},{15,... | collective-permute-start | bytes 3145736 | tf_op jit(solution)/shard_map/ppermute | solution.py:139
  30.8 36.3 %collective-permute-start.4 = (bf16[256,2048]{1,0:T(8,128)(2,1)S(1)}, bf16[256,2048]{1,0:T(8,128)(2,1)}, u32[]{:S(2)}, u32[]{:S(2)}) collective-permute-start(bf16[256,2048]{1,0:T(8,128)(2,1)S(1)} %collective-permute-done.refs_0_.refs_1_), channel_id=1, source_target_pairs={{0,1},{1,0},{2,3},{3,2},{4,5},{5,4},{6,7},{7,6},{8,9},{9,8},{10,11... | collective-permute-start | bytes 3145736 | tf_op jit(solution)/shard_map/ppermute | solution.py:145
  30.8 46.3 %collective-permute-start.3 = (bf16[256,2048]{1,0:T(8,128)(2,1)S(1)}, bf16[256,2048]{1,0:T(8,128)(2,1)}, u32[]{:S(2)}, u32[]{:S(2)}) collective-permute-start(bf16[256,2048]{1,0:T(8,128)(2,1)S(1)} %collective-permute-done.2.refs_2_.refs_3_), channel_id=1, source_target_pairs={{4,0},{5,1},{8,4},{9,5},{12,8},{13,9},{14,12},{15,13},{10,14},{11,... | collective-permute-start | bytes 3145736 | tf_op jit(solution)/shard_map/ppermute | solution.py:142
  31.1 36.0 %collective-permute-start.5 = (bf16[256,2048]{1,0:T(8,128)(2,1)S(1)}, bf16[256,2048]{1,0:T(8,128)(2,1)}, u32[]{:S(2)}, u32[]{:S(2)}) collective-permute-start(bf16[256,2048]{1,0:T(8,128)(2,1)S(1)} %collective-permute-done.2.refs_2_.refs_3_), channel_id=1, source_target_pairs={{0,1},{1,0},{2,3},{3,2},{4,5},{5,4},{6,7},{7,6},{8,9},{9,8},{10,11... | collective-permute-start | bytes 3145736 | tf_op jit(solution)/shard_map/ppermute | solution.py:145
  32.1 26.4 %all-to-all-start = ((f32[16,1,192]{2,1,0:T(1,128)}), f32[16,1,192]{2,1,0:T(1,128)S(1)}, u32[]{:S(2)}, u32[]{:S(2)}) async-start(f32[16,1,192]{2,1,0:T(1,128)} %copy.56), calls=%async_computation | async-start | bytes 32768 | tf_op jit(solution)/shard_map/all_to_all | solution.py:475
  77.7 26.7 %collective-permute-start.7 = (bf16[256,2048]{1,0:T(8,128)(2,1)}, bf16[256,2048]{1,0:T(8,128)(2,1)S(1)}, u32[]{:S(2)}, u32[]{:S(2)}) collective-permute-start(bf16[256,2048]{1,0:T(8,128)(2,1)} %collective-permute-done.1.refs_0_.refs_1_), channel_id=1, source_target_pairs={{0,4},{1,5},{4,8},{5,9},{8,12},{9,13},{12,14},{13,15},{14,10},{15,... | collective-permute-start | bytes 3145736 | tf_op jit(solution)/shard_map/ppermute | solution.py:139
  78.3 30.6 %collective-permute-start.8 = (bf16[256,2048]{1,0:T(8,128)(2,1)}, bf16[256,2048]{1,0:T(8,128)(2,1)}, u32[]{:S(2)}, u32[]{:S(2)}) collective-permute-start(bf16[256,2048]{1,0:T(8,128)(2,1)} %collective-permute-done.3.refs_2_.refs_3_), channel_id=1, source_target_pairs={{4,0},{5,1},{8,4},{9,5},{12,8},{13,9},{14,12},{15,13},{10,14},{11,... | collective-permute-start | bytes 3145736 | tf_op jit(solution)/shard_map/ppermute | solution.py:142
  83.3 53.8 %all-to-all-start.1 = ((bf16[16,96,384]{2,1,0:T(8,128)(2,1)}), bf16[16,96,384]{2,1,0:T(8,128)(2,1)S(1)}, u32[]{:S(2)}, u32[]{:S(2)}) async-start(bf16[16,96,384]{2,1,0:T(8,128)(2,1)} %bitcast.45), calls=%async_computation.1 | async-start | bytes 2359296 | tf_op jit(solution)/shard_map/all_to_all | solution.py:509
  111.3 20.3 %collective-permute-start.11 = (bf16[128,2048]{1,0:T(8,128)(2,1)}, bf16[128,2048]{1,0:T(8,128)(2,1)S(1)}, u32[]{:S(2)}, u32[]{:S(2)}) collective-permute-start(bf16[128,2048]{1,0:T(8,128)(2,1)} %slice.59), channel_id=1, source_target_pairs={{0,4},{1,5},{4,8},{5,9},{8,12},{9,13},{12,14},{13,15},{14,10},{15,... | collective-permute-start | bytes 1572872 | tf_op jit(solution)/shard_map/ppermute | solution.py:139
  113.1 20.5 %collective-permute-start.12 = (bf16[128,2048]{1,0:T(8,128)(2,1)S(1)}, bf16[128,2048]{1,0:T(8,128)(2,1)S(1)}, u32[]{:S(2)}, u32[]{:S(2)}) collective-permute-start(bf16[128,2048]{1,0:T(8,128)(2,1)S(1)} %slice.60), channel_id=1, source_target_pairs={{4,0},{5,1},{8,4},{9,5},{12,8},{13,9},{14,12},{15,13},{10,14},{11,... | collective-permute-start | bytes 1572872 | tf_op jit(solution)/shard_map/ppermute | solution.py:142
  137.1 42.1 %all-to-all-start.2 = ((bf16[16,96,512]{2,1,0:T(8,128)(2,1)}), bf16[16,96,512]{2,1,0:T(8,128)(2,1)S(1)}, u32[]{:S(2)}, u32[]{:S(2)}) async-start(bf16[16,96,512]{2,1,0:T(8,128)(2,1)} %bitcast.44), calls=%async_computation.2 | async-start | bytes 3145728 | tf_op jit(solution)/shard_map/all_to_all | solution.py:509
  179.2 82.9 %all-to-all-start.3 = ((bf16[16,96,512]{2,1,0:T(8,128)(2,1)}), bf16[16,96,512]{2,1,0:T(8,128)(2,1)S(1)}, u32[]{:S(2)}, u32[]{:S(2)}) async-start(bf16[16,96,512]{2,1,0:T(8,128)(2,1)} %bitcast.43), calls=%async_computation.3 | async-start | bytes 3145728 | tf_op jit(solution)/shard_map/all_to_all | solution.py:509
  188.5 37.2 %collective-permute-start.17 = (bf16[1024,768]{1,0:T(8,128)(2,1)}, bf16[1024,768]{1,0:T(8,128)(2,1)}, u32[]{:S(2)}, u32[]{:S(2)}) collective-permute-start(bf16[1024,768]{1,0:T(8,128)(2,1)} %get-tuple-element.153), channel_id=1, source_target_pairs={{0,16},{16,0},{1,17},{17,1},{2,18},{18,2},{3,19},{19,3},{4,20},{20... | collective-permute-start | bytes 4718600 | tf_op jit(solution)/shard_map/ppermute | solution.py:537
  260.7 48.9 %collective-permute-start.18 = (bf16[1024,1024]{1,0:T(8,128)(2,1)}, bf16[1024,1024]{1,0:T(8,128)(2,1)}, u32[]{:S(2)}, u32[]{:S(2)}) collective-permute-start(bf16[1024,1024]{1,0:T(8,128)(2,1)} %get-tuple-element.163), channel_id=1, source_target_pairs={{0,16},{16,0},{1,17},{17,1},{2,18},{18,2},{3,19},{19,3},{4,20},{20... | collective-permute-start | bytes 6291464 | tf_op jit(solution)/shard_map/ppermute | solution.py:537
  283.3 69.8 %collective-permute-start.19 = (bf16[1024,1024]{1,0:T(8,128)(2,1)}, bf16[1024,1024]{1,0:T(8,128)(2,1)}, u32[]{:S(2)}, u32[]{:S(2)}) collective-permute-start(bf16[1024,1024]{1,0:T(8,128)(2,1)} %get-tuple-element.178), channel_id=1, source_target_pairs={{0,16},{16,0},{1,17},{17,1},{2,18},{18,2},{3,19},{19,3},{4,20},{20... | collective-permute-start | bytes 6291464 | tf_op jit(solution)/shard_map/ppermute | solution.py:537
  299.6 53.4 %collective-permute-start.24 = (bf16[128,2048]{1,0:T(8,128)(2,1)}, bf16[128,2048]{1,0:T(8,128)(2,1)S(1)}, u32[]{:S(2)}, u32[]{:S(2)}) collective-permute-start(bf16[128,2048]{1,0:T(8,128)(2,1)} %get-tuple-element.165), channel_id=1, source_target_pairs={{0,1},{1,0},{2,3},{3,2},{4,5},{5,4},{6,7},{7,6},{8,9},{9,8},{10,11... | collective-permute-start | bytes 1572872 | tf_op jit(solution)/shard_map/ppermute | solution.py:145
  299.7 56.7 %collective-permute-start.23 = (bf16[256,2048]{1,0:T(8,128)(2,1)}, bf16[256,2048]{1,0:T(8,128)(2,1)}, u32[]{:S(2)}, u32[]{:S(2)}) collective-permute-start(bf16[256,2048]{1,0:T(8,128)(2,1)} %get-tuple-element.166), channel_id=1, source_target_pairs={{0,1},{1,0},{2,3},{3,2},{4,5},{5,4},{6,7},{7,6},{8,9},{9,8},{10,11... | collective-permute-start | bytes 3145736 | tf_op jit(solution)/shard_map/ppermute | solution.py:145
  356.4 19.8 %collective-permute-start.22 = (bf16[256,2048]{1,0:T(8,128)(2,1)}, bf16[256,2048]{1,0:T(8,128)(2,1)}, u32[]{:S(2)}, u32[]{:S(2)}) collective-permute-start(bf16[256,2048]{1,0:T(8,128)(2,1)} %get-tuple-element.167), channel_id=1, source_target_pairs={{0,1},{1,0},{2,3},{3,2},{4,5},{5,4},{6,7},{7,6},{8,9},{9,8},{10,11... | collective-permute-start | bytes 3145736 | tf_op jit(solution)/shard_map/ppermute | solution.py:145
  366.0 61.1 %collective-permute-start.33 = (bf16[704,2048]{1,0:T(8,128)(2,1)S(1)}, bf16[704,2048]{1,0:T(8,128)(2,1)}, u32[]{:S(2)}, u32[]{:S(2)}) collective-permute-start(bf16[704,2048]{1,0:T(8,128)(2,1)S(1)} %constant_dynamic-slice_fusion), channel_id=1, source_target_pairs={{0,16},{16,0},{1,17},{17,1},{2,18},{18,2},{3,19},{19,3},{4,20},{20... | collective-permute-start | bytes 8650760 | tf_op jit(solution)/shard_map/ppermute | solution.py:563
  367.4 26.5 %collective-permute-start.21 = (bf16[256,2048]{1,0:T(8,128)(2,1)}, bf16[256,2048]{1,0:T(8,128)(2,1)}, u32[]{:S(2)}, u32[]{:S(2)}) collective-permute-start(bf16[256,2048]{1,0:T(8,128)(2,1)} %get-tuple-element.168), channel_id=1, source_target_pairs={{0,1},{1,0},{2,3},{3,2},{4,5},{5,4},{6,7},{7,6},{8,9},{9,8},{10,11... | collective-permute-start | bytes 3145736 | tf_op jit(solution)/shard_map/ppermute | solution.py:145
  381.6 21.9 %collective-permute-start.20 = (bf16[128,2048]{1,0:T(8,128)(2,1)}, bf16[128,2048]{1,0:T(8,128)(2,1)S(1)}, u32[]{:S(2)}, u32[]{:S(2)}) collective-permute-start(bf16[128,2048]{1,0:T(8,128)(2,1)} %get-tuple-element.169), channel_id=1, source_target_pairs={{0,1},{1,0},{2,3},{3,2},{4,5},{5,4},{6,7},{7,6},{8,9},{9,8},{10,11... | collective-permute-start | bytes 1572872 | tf_op jit(solution)/shard_map/ppermute | solution.py:145
  (28 other events, 315.9 us)
where the time goes:
time: 442 us; the launch traced here: 433 us
  Pallas kernels  180 us (41%)
  waiting for transfers between devices  152 us (34%)
  starting transfers between devices  54.9 us (12%)
  other arithmetic  20.8 us (5%)
  local copies, waits for them, and re-layouts  13.1 us (3%)
  matrix products  11 us (2%)
    ppermute x3, waiting for transfers between devices, local(): lax.ppermute(sent[(d - 1) * piece:d * piece], 'dp', shifts[d])  57.2 us
    pallas_call x3, Pallas kernels, chunk_grads(): pl.pallas_call(body, out_shape=(jax.ShapeDtypeStruct((n_slots, w), bf16),...  50.1 us
    pallas_call x5, Pallas kernels, put_rows(): pl.pallas_call(body, out_shape=(jax.ShapeDtypeStruct((n_slots, width), bf...  43.1 us
    ppermute x8, waiting for transfers between devices, ahead(): return lax.ppermute(x, 'expert', self.fwd)  39.6 us
    pallas_call x2, Pallas kernels, spread_back(): pl.pallas_call(body, out_shape=[jax.ShapeDtypeStruct((h * tok_rows, width...  31.3 us
    all_to_all x3, starting transfers between devices, send_chunk(): lax.all_to_all(part, 'expert', split_axis=0, concat_axis=0, tiled=True)  23.6 us
    pallas_call x3, Pallas kernels, own_half(): pl.pallas_call(body, out_shape=jax.ShapeDtypeStruct((piece, w), bf16), gr...  21.7 us
    pallas_call x3, Pallas kernels, down_rows(): pl.pallas_call(body, out_shape=jax.ShapeDtypeStruct((hidden_width, width)...  21.1 us
  transfers between devices with their start and end apart: 38, of which 18 were waited for; matrix products, arithmetic and copies ran while one was open for 8% of the time, Pallas kernels for 42%

commit v1 on v0

--- a/solution.py
+++ b/solution.py
@@ -20,9 +20,11 @@
 
 def chunk_widths(width):
     lanes = width // 128
-    shares = (3, 7, 11)
-    ends = [-(-lanes * x // 11) * 128 for x in shares]
-    return [e - s for s, e in zip([0] + ends, ends) if e > s]
+    if lanes < 8:
+        return [[width]]
+    ends = [-(-lanes * x // 11) * 128 for x in (0, 2, 5, 8, 11)]
+    sizes = [e - s for s, e in zip(ends, ends[1:])]
+    return [sizes[:2], sizes[2:]]
 
 
 def chip_cycle(n_chips):
@@ -147,6 +149,7 @@
 
 def gather_rows(ring, tokens, out_grad, table, cap, up_mat, down_mat, first_width, beside):
     tok_rows = tokens.shape[0]
+    beside = list(beside)
     own = jnp.concatenate([tokens, out_grad], axis=0)
 
     def whole(x):
@@ -157,18 +160,20 @@
 
     state = None
     ahead, behind = own, own
-    pending = ([ring.at(0, False), ring.at(0, True)], [whole(own), whole(ring.other_core(own))])
+    pending = [([ring.at(0, False), ring.at(0, True)], [whole(own), whole(ring.other_core(own))])]
     for d in range(1, ring.far):
         ahead, behind = ring.ahead(ahead), ring.behind(behind)
-        if d >= 2:
-            for spots, shards in pending:
+        if d == 1:
+            ahead, behind, table = lax.optimization_barrier((ahead, behind, table))
+        else:
+            now, pending = (pending[:1], pending[1:]) if d == 2 else (pending, [])
+            for spots, shards in now:
                 state = place(spots, shards, state)
-            pending = []
             ahead, behind, state = lax.optimization_barrier((ahead, behind, state))
-            if d == 2:
-                ahead, behind, beside = lax.optimization_barrier((ahead, behind, beside))
-        else:
-            pending = [pending]
+            if d - 2 < len(beside):
+                ahead, behind, beside[d - 2] = lax.optimization_barrier(
+                    (ahead, behind, beside[d - 2])
+                )
         pending.append(
             (
                 [ring.at(d, False), ring.at(-d, False), ring.at(d, True), ring.at(-d, True)],
@@ -177,8 +182,6 @@
         )
     far_tok = ring.ahead(ahead[:tok_rows])
     far_grad = ring.behind(behind[tok_rows:])
-    if ring.far == 1:
-        pending = [pending]
     for spots, shards in pending:
         state = place(spots, shards, state)
     far_tok, far_grad, state = lax.optimization_barrier((far_tok, far_grad, state))
@@ -191,48 +194,75 @@
     return state, (theirs_tok, theirs_grad), beside
 
 
+def add_blocks(blocks, tok_rows, split):
+    width = blocks[0][0][0].shape[1]
+    operands = [x for terms in blocks for x in terms]
+    half = tok_rows // 2
+
+    def body(*refs):
+        outs, at = refs[len(operands) :], 0
+        for i, terms in enumerate(blocks):
+            for lower in (0, half):
+                total = jnp.zeros((half, width), f32)
+                for j, (_, _, rows, first) in enumerate(terms):
+                    if first <= lower < first + rows:
+                        total += refs[at + j][lower - first : lower - first + half, :].astype(f32)
+                if split:
+                    outs[1 if lower else 0][...] = total.astype(bf16)
+                else:
+                    outs[i][lower : lower + half, :] = total.astype(bf16)
+            at += len(terms)
+
+    height, count = (half, 2) if split else (tok_rows, len(blocks))
+    out = pl.pallas_call(
+        body,
+        out_shape=[jax.ShapeDtypeStruct((height, width), bf16)] * count,
+        grid=(1,),
+        in_specs=[
+            pl.BlockSpec((rows, width), lambda i, at=at: (at, 0)) for _, at, rows, _ in operands
+        ],
+        out_specs=[pl.BlockSpec((height, width), lambda i: (0, 0))] * count,
+        compiler_params=pltpu.CompilerParams(vmem_limit_bytes=KERNEL_VMEM),
+        cost_estimate=LIGHT,
+        name="add_blocks",
+    )(*[x for x, _, _, _ in operands])
+    return list(out)
+
+
 def sum_back(ring, theirs, mine, tok_rows, fills):
-    handed, ours = {}, {}
+    terms = {}
     j = 0
     for piece, own in zip(theirs, mine):
         piece = ring.other_core(piece)
-        for at in range(0, piece.shape[0], tok_rows):
-            handed[ring.names[j]] = piece[at : at + tok_rows]
-            ours[ring.names[j]] = own[at : at + tok_rows]
+        for at in range(piece.shape[0] // tok_rows):
+            terms[ring.names[j]] = [(own, at, tok_rows, 0), (piece, at, tok_rows, 0)]
             j += 1
 
-    def plus(d, *others):
-        total = ours[d].astype(f32) + handed[d].astype(f32)
-        for x in others:
-            total = total + x.astype(f32)
-        return total.astype(bf16)
-
     half = tok_rows // 2
-    first = plus(ring.far)
-    top, low = ring.ahead(first[:half]), ring.behind(first[half:])
-    none = jnp.zeros_like(top)
-    ahead = jnp.concatenate([top, none], axis=0)
-    behind = jnp.concatenate([none, low], axis=0)
-    mark, filled = (top, low), []
+    top, low = add_blocks([terms[ring.far]], tok_rows, True)
+    ahead, behind = (ring.ahead(top), 0, half, 0), (ring.behind(low), 0, half, half)
+    mark, filled = (ahead[0], behind[0]), []
     for d in range(ring.far - 1, 0, -1):
-        ahead, behind = ring.ahead(plus(-d, ahead)), ring.behind(plus(d, behind))
+        ahead, behind = add_blocks([terms[-d] + [ahead], terms[d] + [behind]], tok_rows, False)
+        ahead, behind = ring.ahead(ahead), ring.behind(behind)
         if len(filled) < len(fills):
             done = fills[len(filled)](mark)
             ahead, behind, done = lax.optimization_barrier((ahead, behind, done))
             filled.append(done)
         mark = (ahead, behind)
+        ahead, behind = (ahead, 0, tok_rows, 0), (behind, 0, tok_rows, 0)
     for fill in fills[len(filled) :]:
         filled.append(fill(mark))
-    return plus(0, ahead, behind), filled
+    return add_blocks([terms[0] + [ahead, behind]], tok_rows, False)[0], filled
 
 
 def blocks_per_step(n_blocks, cap):
     return max(b for b in range(1, n_blocks + 1) if n_blocks % b == 0 and b * cap <= 768)
 
 
-def chunk_grads(order, cols, rows, routed, gate, up_mat, down_mat, start, piece, ready):
+def chunk_grads(order, cols, rows, routed, gate, gate_at, w, up_mat, down_mat, start, piece, ready):
     n_slots, width = rows.shape
-    n_peers, cap, w = gate.shape
+    n_peers, cap, _ = gate.shape
     n = blocks_per_step(n_peers, cap)
     r = n * cap
     n_rows, n_cols = n_slots // r, cols.shape[0]
@@ -300,7 +330,10 @@
             in_specs=in_specs
             + [pl.BlockSpec((n_slots, piece), lambda i, order, cols: (0, cols[col(i)]))]
             + [
-                pl.BlockSpec((1, cap, w), lambda i, order, cols, b=b: (order[n * row(i) + b], 0, 0))
+                pl.BlockSpec(
+                    (pl.Element(1), pl.Element(cap), pl.Element(w)),
+                    lambda i, order, cols, b=b: (order[n * row(i) + b], 0, gate_at),
+                )
                 for b in range(n)
             ],
             out_specs=(
@@ -481,16 +514,22 @@
     )
     ring = Ring()
     table = table.reshape(n_peers, 2, cap)[ring.order]
-    widths = chunk_widths(hidden_width)
+    groups = chunk_widths(hidden_width)
+    widths = [w for group_widths in groups for w in group_widths]
     starts = [sum(widths[:i]) for i in range(len(widths))]
+    spans = [sum(group_widths) for group_widths in groups]
+    offsets = [sum(spans[:i]) for i in range(len(spans))]
     route_gates = jnp.transpose(gate_saved, (1, 0, 2)).reshape(n_routes, hidden_width)
     route_of = (tok_of + tok_rows * choice_of).astype(i32).reshape(n_slots, 1)
     pick = (route_of == jnp.arange(n_routes, dtype=i32)[None, :]).astype(bf16)
     send_gate = [
         dot(pick, route_gates[:, s : s + w], ((1,), (0,))).astype(bf16).reshape(n_peers, cap, w)
-        for s, w in zip(starts, widths)
+        for s, w in zip(offsets, spans)
     ]
-    (rows_in, routed, up_first, grad_first), mark, send_gate[1:] = gather_rows(
+    def exchange(part):
+        return lax.all_to_all(part, "expert", split_axis=0, concat_axis=0, tiled=True)
+
+    (rows_in, routed, up_first, grad_first), mark, (_, (recv_gate, rest)) = gather_rows(
         ring,
         tokens,
         out_grad,
@@ -499,32 +538,46 @@
         up_mat,
         down_mat,
         widths[0],
-        send_gate[1:],
+        [send_gate[:1], ([exchange(send_gate[0])], send_gate[1:])],
     )
-
-    def send_chunk(i, mark):
-        part = send_gate[i]
-        if mark is not None:
-            part, _ = lax.optimization_barrier((part, mark))
-        return lax.all_to_all(part, "expert", split_axis=0, concat_axis=0, tiled=True)
-
-    recv_gate = [send_chunk(i, mark) for i, mark in zip(range(len(widths)), (None, mark))]
+    rest, _ = lax.optimization_barrier((rest, mark))
+    recv_gate = recv_gate + [exchange(part) for part in rest]
+    gate_of = [
+        (recv_gate[i], sum(group_widths[:j]))
+        for i, group_widths in enumerate(groups)
+        for j in range(len(group_widths))
+    ]
 
     piece = model_width // n_dp
     shifts = [[(i, (i + d) % n_dp) for i in range(n_dp)] for d in range(n_dp)]
 
     peer_cols = lax.rem(group + jnp.arange(1, n_dp, dtype=i32), n_dp)
     own_cols = group.reshape(1).astype(i32)
-    both_parts, arrivals, own_parts = [], [], []
-    sum_down = None
+    both_parts, hidden_parts, arrivals = [], [], []
+    own_parts, sum_down = [], None
+    early = len(groups[0])
     rows_now, routed_now = rows_in, routed
     for c, w in enumerate(widths):
+        if c == early:
+            for e in range(early):
+                own_parts.append(own_half(own_cols, rows_now, both_parts[e], piece))
+                sum_down = down_rows(
+                    routed_now, hidden_parts[e], starts[e], sum_down, hidden_width
+                )
+            rows_now, routed_now, own_parts, sum_down = lax.optimization_barrier(
+                (rows_now, routed_now, own_parts, sum_down)
+            )
+        if c >= 2:
+            rows_now, arrivals[c - 2] = lax.optimization_barrier((rows_now, arrivals[c - 2]))
+        gate, gate_at = gate_of[c]
         hidden, both, sent = chunk_grads(
             ring.order,
             peer_cols,
             rows_now,
             routed_now,
-            recv_gate[c],
+            gate,
+            gate_at,
+            w,
             up_mat,
             down_mat,
             starts[c],
@@ -532,56 +585,55 @@
             (up_first, grad_first) if c == 0 else None,
         )
         both_parts.append(both)
+        hidden_parts.append(hidden)
         arrivals.append(
             [
                 lax.ppermute(sent[(d - 1) * piece : d * piece], "dp", shifts[d])
                 for d in range(1, n_dp)
             ]
         )
-        if c + 1 < len(widths):
-            own = own_half(own_cols, rows_now, both, piece)
-            sum_down = down_rows(routed_now, hidden, starts[c], sum_down, hidden_width)
-            if c + 2 < len(widths):
-                recv_gate.append(send_chunk(c + 2, own))
-            if c >= 1:
-                rows_now, arrivals[c - 1] = lax.optimization_barrier((rows_now, arrivals[c - 1]))
-            rows_now, routed_now, own, sum_down = lax.optimization_barrier(
-                (rows_now, routed_now, own, sum_down)
-            )
-            own_parts.append(own)
+        rows_now, routed_now, _ = lax.optimization_barrier((rows_now, routed_now, sent))
 
     heights = [1] + [2] * (ring.far - 1) + [1]
     theirs = spread_back(both_parts, starts, gate_mat, up_mat, table, tok_rows, True, heights)
-    hidden, _ = lax.optimization_barrier((hidden, theirs))
-    sum_down = down_rows(routed_now, hidden, starts[-1], sum_down, hidden_width)
+    late = list(range(min(early, len(widths)), len(widths)))
+    for c in late:
+        hidden, _ = lax.optimization_barrier((hidden_parts[c], theirs))
+        sum_down = down_rows(routed_now, hidden, starts[c], sum_down, hidden_width)
+    if not late:
+        own_parts = [own_half(own_cols, rows_now, x, piece) for x in both_parts]
+        for c, hidden in enumerate(hidden_parts):
+            sum_down = down_rows(routed_now, hidden, starts[c], sum_down, hidden_width)
     low = hidden_width // n_dp
     sent = [
         lax.dynamic_slice_in_dim(sum_down, lax.rem(group + d, n_dp) * low, low, 0)
         for d in range(1, n_dp)
     ]
-    last, arrivals[:-1], sent = lax.optimization_barrier((both, arrivals[:-1], sent))
+    last, arrivals[:-1], sent = lax.optimization_barrier((both_parts[-1], arrivals[:-1], sent))
     arrived = [lax.ppermute(part, "dp", shifts[d]) for d, part in enumerate(sent, 1)]
     mine = spread_back(
         both_parts[:-1] + [last], starts, gate_mat, up_mat, table, tok_rows, False, heights
     )
     mine, arrivals[-1] = lax.optimization_barrier((mine, arrivals[-1]))
 
-    def last_half(mark):
-        held, _ = lax.optimization_barrier((both, mark))
-        return own_half(own_cols, rows_now, held, piece), arrivals[-1]
-
-    def join_first(mark):
+    def late_halves(mark):
+        parts, _ = lax.optimization_barrier((both_parts, mark))
+        return [own_half(own_cols, rows_now, parts[c], piece) for c in late]
+
+    def join_early(mark):
         parts, _ = lax.optimization_barrier((own_parts, mark))
         joined = None
         for c, part in enumerate(parts):
             joined = join_halves(part, arrivals[c], starts[c], joined, hidden_width)
         return joined
 
-    input_grad, ((own, arrivals[-1]), totals) = sum_back(
-        ring, theirs, mine, tok_rows, [last_half, join_first]
+    input_grad, (late_parts, totals) = sum_back(
+        ring, theirs, mine, tok_rows, [late_halves, join_early]
     )
     arrived, _ = lax.optimization_barrier((arrived, input_grad))
-    grad_gate, grad_up = join_halves(own, arrivals[-1], starts[-1], totals, hidden_width)
+    for c, part in zip(late, late_parts):
+        totals = join_halves(part, arrivals[c], starts[c], totals, hidden_width)
+    grad_gate, grad_up = totals
     down = lax.dynamic_slice_in_dim(sum_down, group * low, low, 0).astype(f32)
     for part in arrived:
         down = down + part.astype(f32)

time: 442 us -> 407 us (0.921)
  waiting for transfers between devices: 152 us -> 97.6 us
  Pallas kernels: 180 us -> 213 us
  other arithmetic: 20.8 us -> 9.06 us
  local copies, waits for them, and re-layouts: 13.1 us -> 19.3 us
    ppermute x3 -> x4, waiting for transfers between devices: 57.2 us -> 0.01 us  [local(): lax.ppermute(sent[(d - 1) * piece:d * piece], 'dp', shifts[d])]
    ppermute x8, waiting for transfers between devices: 39.6 us -> 84.4 us  [ahead(): return lax.ppermute(x, 'expert', self.fwd)]
    all_to_all x3 -> x2, starting transfers between devices: 23.6 us -> 9.45 us  [exchange(): lax.all_to_all(part, 'expert', split_axis=0, concat_axis=0, tiled=True)]
    ppermute x1, waiting for transfers between devices: 13.6 us -> 0.01 us  [local(): lax.ppermute(part, 'dp', shifts[d])]
    pallas_call x0 -> x5, Pallas kernels: none -> 13.5 us  [add_blocks(): pl.pallas_call(body, out_shape=[jax.ShapeDtypeStruct((height, width), bf1...]
    pallas_call x3 -> x4, Pallas kernels: 50.1 us -> 62.7 us  [chunk_grads(): pl.pallas_call(body, out_shape=(jax.ShapeDtypeStruct((n_slots, w), bf16),...]
    convert_element_type x5 -> x0, other arithmetic: 11.8 us -> none  [plus(): return total.astype(bf16)]
    ppermute x8, waiting for transfers between devices: 20.1 us -> 9.18 us  [behind(): return lax.ppermute(x, 'expert', self.bwd)]
  transfers between devices with their start and end apart: 38 -> 38, of which waited for: 18 -> 17; matrix products, arithmetic and copies ran while one was open for 8% -> 5% of each run, Pallas kernels for 42% -> 53%
where the time goes in v1:
time: 407 us; the launch traced here: 402 us
  Pallas kernels  213 us (52%)
  waiting for transfers between devices  97.6 us (24%)
  starting transfers between devices  52.2 us (13%)
  local copies, waits for them, and re-layouts  19.3 us (5%)
  matrix products  9.61 us (2%)
  other arithmetic  9.06 us (2%)
    ppermute x8, waiting for transfers between devices, ahead(): return lax.ppermute(x, 'expert', self.fwd)  84.4 us
    pallas_call x4, Pallas kernels, chunk_grads(): pl.pallas_call(body, out_shape=(jax.ShapeDtypeStruct((n_slots, w), bf16),...  62.7 us
    pallas_call x5, Pallas kernels, put_rows(): pl.pallas_call(body, out_shape=(jax.ShapeDtypeStruct((n_slots, width), bf...  37.5 us
    pallas_call x2, Pallas kernels, spread_back(): pl.pallas_call(body, out_shape=[jax.ShapeDtypeStruct((h * tok_rows, width...  35 us
    pallas_call x4, Pallas kernels, own_half(): pl.pallas_call(body, out_shape=jax.ShapeDtypeStruct((piece, w), bf16), gr...  24.6 us
    pallas_call x4, Pallas kernels, down_rows(): pl.pallas_call(body, out_shape=jax.ShapeDtypeStruct((hidden_width, width)...  24.2 us
    ppermute x8, starting transfers between devices, ahead(): return lax.ppermute(x, 'expert', self.fwd)  21.5 us
    pallas_call x4, Pallas kernels, join_halves(): pl.pallas_call(body, out_shape=(shape, shape), grid=(piece // r,), in_spe...  15.3 us
  transfers between devices with their start and end apart: 38, of which 17 were waited for; matrix products, arithmetic and copies ran while one was open for 5% of the time, Pallas kernels for 53%

profile of v1, /device:TPU:0, one launch (start us, length us, event | category | flops | bytes accessed | tf_op | source)
XLA Modules:
  0.0 401.6 jit_solution(1117314864331081062)
XLA Ops:
  4.1 7.4 %all-to-all-start = ((f32[16,1,192]{2,1,0:T(1,128)}), f32[16,1,192]{2,1,0:T(1,128)S(1)}, u32[]{:S(2)}, u32[]{:S(2)}) async-start(f32[16,1,192]{2,1,0:T(1,128)} %copy.59), calls=%async_computation | async-start | bytes 32768 | tf_op jit(solution)/shard_map/all_to_all | solution.py:508
  27.1 50.6 %collective-permute-done.refs_0_.refs_1_ = bf16[256,2048]{1,0:T(8,128)(2,1)} collective-permute-done((bf16[256,2048]{1,0:T(8,128)(2,1)S(1)}, bf16[256,2048]{1,0:T(8,128)(2,1)}, u32[]{:S(2)}, u32[]{:S(2)}) %collective-permute-start) | collective-permute-done | bytes 1048608 | tf_op jit(solution)/shard_map/ppermute | solution.py:141
  79.8 12.1 %collective-permute-start.2 = (bf16[256,2048]{1,0:T(8,128)(2,1)}, bf16[256,2048]{1,0:T(8,128)(2,1)}, u32[]{:S(2)}, u32[]{:S(2)}) collective-permute-start(bf16[256,2048]{1,0:T(8,128)(2,1)} %collective-permute-done.refs_0_.refs_1_), channel_id=1, source_target_pairs={{0,4},{1,5},{4,8},{5,9},{8,12},{9,13},{12,14},{13,15},{14,10},{15,... | collective-permute-start | bytes 3145736 | tf_op jit(solution)/shard_map/ppermute | solution.py:141
  93.6 5.8 %put_rows.5 = (bf16[1536,2048]{1,0:T(8,128)(2,1)}, bf16[1536,2048]{1,0:T(8,128)(2,1)}, f32[1536,256]{1,0:T(8,128)}, f32[1536,256]{1,0:T(8,128)}) custom-call(s32[2]{0:T(128)} %constant.64.clone.spots_ref, f32[16,96,2]{2,1,0:T(8,128)} %copy.64.table_ref, bf16[2048,1408]{1,0:T(8,128)(2,1)} %bitcast.22, bf16[1408,2048]{1,0:T(8,128)(2,1)} %bitcast.32, ...), custom_call_target="tpu_custom_call" | custom-call | flops 1000 | bytes 1000 | tf_op jit(solution)/shard_map/put_rows/pallas_call | solution.py:88
  99.4 15.0 %collective-permute-done.2.refs_0_.refs_1_ = bf16[256,2048]{1,0:T(8,128)(2,1)} collective-permute-done((bf16[256,2048]{1,0:T(8,128)(2,1)}, bf16[256,2048]{1,0:T(8,128)(2,1)}, u32[]{:S(2)}, u32[]{:S(2)}) %collective-permute-start.2) | collective-permute-done | bytes 1048608 | tf_op jit(solution)/shard_map/ppermute | solution.py:141
  124.5 8.6 %put_rows.6 = (bf16[1536,2048]{1,0:T(8,128)(2,1)}, bf16[1536,2048]{1,0:T(8,128)(2,1)}, f32[1536,256]{1,0:T(8,128)}, f32[1536,256]{1,0:T(8,128)}) custom-call(s32[4]{0:T(128)} %constant.65.clone.spots_ref, f32[16,96,2]{2,1,0:T(8,128)} %copy.64.table_ref, ...), custom_call_target="tpu_custom_call", output_to_operand_aliasing={{0}: (12, {}), {1}: (13, {}), {2}: (14, {}), {3}: (15, {})} | custom-call | flops 1000 | bytes 1000 | tf_op jit(solution)/shard_map/put_rows/pallas_call | solution.py:88
  133.2 8.6 %put_rows.7 = (bf16[1536,2048]{1,0:T(8,128)(2,1)}, bf16[1536,2048]{1,0:T(8,128)(2,1)}, f32[1536,256]{1,0:T(8,128)}, f32[1536,256]{1,0:T(8,128)}) custom-call(s32[4]{0:T(128)} %constant.66.clone.spots_ref, f32[16,96,2]{2,1,0:T(8,128)} %copy.64.table_ref, ...), custom_call_target="tpu_custom_call", output_to_operand_aliasing={{0}: (12, {}), {1}: (13, {}), {2}: (14, {}), {3}: (15, {})} | custom-call | flops 1000 | bytes 1000 | tf_op jit(solution)/shard_map/put_rows/pallas_call | solution.py:88
  149.7 8.6 %put_rows.8 = (bf16[1536,2048]{1,0:T(8,128)(2,1)}, bf16[1536,2048]{1,0:T(8,128)(2,1)}, f32[1536,256]{1,0:T(8,128)}, f32[1536,256]{1,0:T(8,128)}) custom-call(s32[4]{0:T(128)} %constant.67.clone.spots_ref, f32[16,96,2]{2,1,0:T(8,128)} %copy.64.table_ref, ...), custom_call_target="tpu_custom_call", output_to_operand_aliasing={{0}: (12, {}), {1}: (13, {}), {2}: (14, {}), {3}: (15, {})} | custom-call | flops 1000 | bytes 1000 | tf_op jit(solution)/shard_map/put_rows/pallas_call | solution.py:88
  169.8 5.7 %put_rows.9 = (bf16[1536,2048]{1,0:T(8,128)(2,1)}, bf16[1536,2048]{1,0:T(8,128)(2,1)}, f32[1536,256]{1,0:T(8,128)}, f32[1536,256]{1,0:T(8,128)}) custom-call(s32[2]{0:T(128)} %constant.68.clone.spots_ref, f32[16,96,2]{2,1,0:T(8,128)} %copy.64.table_ref, ...), custom_call_target="tpu_custom_call", output_to_operand_aliasing={{0}: (8, {}), {1}: (9, {}), {2}: (10, {}), {3}: (11, {})} | custom-call | flops 1000 | bytes 1000 | tf_op jit(solution)/shard_map/put_rows/pallas_call | solution.py:88
  175.6 8.0 %chunk_grads.4 = (bf16[1536,256]{1,0:T(8,128)(2,1)}, bf16[1536,512]{1,0:T(8,128)(2,1)}, bf16[1024,512]{1,0:T(8,128)(2,1)}) custom-call(s32[16]{0:T(128)} %fusion.12.order_ref, s32[1]{0:T(128)S(6)} %rem.31.cols_ref, f32[1536,256]{1,0:T(8,128)} %get-tuple-element.174.refs_0_, f32[1536,256]{1,0:T(8,128)} %get-tuple-element.175.refs_1_, ...), custom_call_target="tpu_custom_call" | custom-call | flops 1000 | bytes 1000 | tf_op jit(solution)/shard_map/chunk_grads/pallas_call | solution.py:320
  185.1 18.3 %chunk_grads.5 = (bf16[1536,384]{1,0:T(8,128)(2,1)}, bf16[1536,768]{1,0:T(8,128)(2,1)}, bf16[1024,768]{1,0:T(8,128)(2,1)}) custom-call(s32[16]{0:T(128)} %fusion.12.order_ref, s32[1]{0:T(128)S(6)} %rem.31.cols_ref, bf16[1536,2048]{1,0:T(8,128)(2,1)} %get-tuple-element.229.refs_2_.refs_0_.refs_4_.rows_ref, ...), custom_call_target="tpu_custom_call" | custom-call | flops 1000 | bytes 1000 | tf_op jit(solution)/shard_map/chunk_grads/pallas_call | solution.py:320
  209.1 6.5 %own_half.5.refs_0_ = bf16[1024,768]{1,0:T(8,128)(2,1)} custom-call(s32[1]{0:T(128)} %bitcast.1.cols_ref, bf16[1536,2048]{1,0:T(8,128)(2,1)} %get-tuple-element.229.refs_2_.refs_0_.refs_4_.rows_ref, bf16[1536,768]{1,0:T(8,128)(2,1)} %get-tuple-element.183.both_ref.refs_1_), custom_call_target="tpu_custom_call" | custom-call | flops 1000 | bytes 1000 | tf_op jit(solution)/shard_map/own_half/pallas_call | solution.py:359
  215.6 5.3 %down_rows.4.refs_0_ = bf16[1408,2048]{1,0:T(8,128)(2,1)} custom-call(bf16[1536,2048]{1,0:T(8,128)(2,1)} %get-tuple-element.203.refs_1_.routed_ref, bf16[1536,256]{1,0:T(8,128)(2,1)} %get-tuple-element.188.hidden_ref), custom_call_target="tpu_custom_call" | custom-call | flops 1000 | bytes 1000 | tf_op jit(solution)/shard_map/down_rows/pallas_call | solution.py:392
  220.9 6.3 %down_rows.5.refs_0_ = bf16[1408,2048]{1,0:T(8,128)(2,1)} custom-call(bf16[1536,2048]{1,0:T(8,128)(2,1)} %get-tuple-element.203.refs_1_.routed_ref, bf16[1536,384]{1,0:T(8,128)(2,1)} %get-tuple-element.187.hidden_ref, bf16[1408,2048]{1,0:T(8,128)(2,1)} %down_rows.4.refs_0_), custom_call_target="tpu_custom_call", output_to_operand_aliasing={{}: (2, {})} | custom-call | flops 1000 | bytes 1000 | tf_op jit(solution)/shard_map/down_rows/pallas_call | solution.py:392
  228.7 18.2 %chunk_grads.6 = (bf16[1536,384]{1,0:T(8,128)(2,1)}, bf16[1536,768]{1,0:T(8,128)(2,1)}, bf16[1024,768]{1,0:T(8,128)(2,1)}) custom-call(s32[16]{0:T(128)} %fusion.12.order_ref, s32[1]{0:T(128)S(6)} %rem.31.cols_ref, bf16[1536,2048]{1,0:T(8,128)(2,1)} %get-tuple-element.229.refs_2_.refs_0_.refs_4_.rows_ref, ...), custom_call_target="tpu_custom_call" | custom-call | flops 1000 | bytes 1000 | tf_op jit(solution)/shard_map/chunk_grads/pallas_call | solution.py:320
  248.5 18.2 %chunk_grads.7 = (bf16[1536,384]{1,0:T(8,128)(2,1)}, bf16[1536,768]{1,0:T(8,128)(2,1)}, bf16[1024,768]{1,0:T(8,128)(2,1)}) custom-call(s32[16]{0:T(128)} %fusion.12.order_ref, s32[1]{0:T(128)S(6)} %rem.31.cols_ref, bf16[1536,2048]{1,0:T(8,128)(2,1)} %get-tuple-element.229.refs_2_.refs_0_.refs_4_.rows_ref, ...), custom_call_target="tpu_custom_call" | custom-call | flops 1000 | bytes 1000 | tf_op jit(solution)/shard_map/chunk_grads/pallas_call | solution.py:320
  267.3 17.7 %spread_back.2 = (bf16[128,2048]{1,0:T(8,128)(2,1)}, bf16[256,2048]{1,0:T(8,128)(2,1)}, bf16[256,2048]{1,0:T(8,128)(2,1)}, bf16[256,2048]{1,0:T(8,128)(2,1)}, bf16[128,2048]{1,0:T(8,128)(2,1)}) custom-call(bf16[1536,512]{1,0:T(8,128)(2,1)} %get-tuple-element.178.both_ref.refs_0_, bf16[1536,768]{1,0:T(8,128)(2,1)} %get-tuple-element.183.both_ref.refs_1_, ...), custom_call_target="tpu_custom_call" | custom-call | flops 1000 | bytes 1000 | tf_op jit(solution)/shard_map/spread_back/pallas_call | solution.py:466
  285.1 6.3 %down_rows.6.refs_0_ = bf16[1408,2048]{1,0:T(8,128)(2,1)} custom-call(bf16[1536,2048]{1,0:T(8,128)(2,1)} %get-tuple-element.203.refs_1_.routed_ref, bf16[1536,384]{1,0:T(8,128)(2,1)} %get-tuple-element.212.hidden_ref, bf16[1408,2048]{1,0:T(8,128)(2,1)} %down_rows.5.refs_0_), custom_call_target="tpu_custom_call", output_to_operand_aliasing={{}: (2, {})} | custom-call | flops 1000 | bytes 1000 | tf_op jit(solution)/shard_map/down_rows/pallas_call | solution.py:392
  291.3 6.3 %down_rows.7 = bf16[1408,2048]{1,0:T(8,128)(2,1)} custom-call(bf16[1536,2048]{1,0:T(8,128)(2,1)} %get-tuple-element.203.refs_1_.routed_ref, bf16[1536,384]{1,0:T(8,128)(2,1)} %get-tuple-element.210.hidden_ref, bf16[1408,2048]{1,0:T(8,128)(2,1)} %down_rows.6.refs_0_), custom_call_target="tpu_custom_call", output_to_operand_aliasing={{}: (2, {})} | custom-call | flops 1000 | bytes 1000 | tf_op jit(solution)/shard_map/down_rows/pallas_call | solution.py:392
  303.4 17.3 %spread_back.3 = (bf16[128,2048]{1,0:T(8,128)(2,1)}, bf16[256,2048]{1,0:T(8,128)(2,1)}, bf16[256,2048]{1,0:T(8,128)(2,1)}, bf16[256,2048]{1,0:T(8,128)(2,1)}, bf16[128,2048]{1,0:T(8,128)(2,1)}) custom-call(bf16[1536,512]{1,0:T(8,128)(2,1)} %get-tuple-element.178.both_ref.refs_0_, bf16[1536,768]{1,0:T(8,128)(2,1)} %get-tuple-element.183.both_ref.refs_1_, ...), custom_call_target="tpu_custom_call" | custom-call | flops 1000 | bytes 1000 | tf_op jit(solution)/shard_map/spread_back/pallas_call | solution.py:466
  324.8 7.1 %collective-permute-done.26.refs_2_ = bf16[64,2048]{1,0:T(8,128)(2,1)S(1)} collective-permute-done((bf16[64,2048]{1,0:T(8,128)(2,1)}, bf16[64,2048]{1,0:T(8,128)(2,1)S(1)}, u32[]{:S(2)}, u32[]{:S(2)}) %collective-permute-start.26) | collective-permute-done | bytes 262176 | tf_op jit(solution)/shard_map/ppermute | solution.py:141
  339.1 6.5 %own_half.6.refs_0_ = bf16[1024,768]{1,0:T(8,128)(2,1)} custom-call(s32[1]{0:T(128)} %bitcast.1.cols_ref, bf16[1536,2048]{1,0:T(8,128)(2,1)} %get-tuple-element.229.refs_2_.refs_0_.refs_4_.rows_ref, bf16[1536,768]{1,0:T(8,128)(2,1)} %get-tuple-element.230.refs_2_.both_ref), custom_call_target="tpu_custom_call" | custom-call | flops 1000 | bytes 1000 | tf_op jit(solution)/shard_map/own_half/pallas_call | solution.py:359
  345.6 6.6 %own_half.7.refs_0_ = bf16[1024,768]{1,0:T(8,128)(2,1)} custom-call(s32[1]{0:T(128)} %bitcast.1.cols_ref, bf16[1536,2048]{1,0:T(8,128)(2,1)} %get-tuple-element.229.refs_2_.refs_0_.refs_4_.rows_ref, bf16[1536,768]{1,0:T(8,128)(2,1)} %get-tuple-element.231.refs_3_.both_ref), custom_call_target="tpu_custom_call" | custom-call | flops 1000 | bytes 1000 | tf_op jit(solution)/shard_map/own_half/pallas_call | solution.py:359
  395.7 5.7 %fusion.4 = bf16[1,704,2048]{2,1,0:T(8,128)(2,1)} fusion(bf16[704,2048]{1,0:T(8,128)(2,1)} %collective-permute-done.34, bf16[1408,2048]{1,0:T(8,128)(2,1)} %down_rows.7, s32[]{:T(128)S(6)} %select_n.46), kind=kLoop, calls=%fused_computation.7 | loop fusion | flops 7208960 | bytes 8650756 | tf_op jit(solution)/shard_map/broadcast_in_dim | solution.py:640
  (162 shorter events, 123.7 us)
Async XLA Ops:
  17.9 125.4 %all-to-all-start.1 = ((bf16[16,96,640]{2,1,0:T(8,128)(2,1)}), bf16[16,96,640]{2,1,0:T(8,128)(2,1)S(1)}, u32[]{:S(2)}, u32[]{:S(2)}) async-start(bf16[16,96,640]{2,1,0:T(8,128)(2,1)} %bitcast.45), calls=%async_computation.1 | async-start | bytes 3932160 | tf_op jit(solution)/shard_map/all_to_all | solution.py:530
  23.6 54.1 %collective-permute-start = (bf16[256,2048]{1,0:T(8,128)(2,1)S(1)}, bf16[256,2048]{1,0:T(8,128)(2,1)}, u32[]{:S(2)}, u32[]{:S(2)}) collective-permute-start(bf16[256,2048]{1,0:T(8,128)(2,1)S(1)} %constant_dynamic-update-slice_fusion.refs_0_.refs_1_), channel_id=1, source_target_pairs={{0,4},{1,5},{4,8},{5,9},{8,12},{9,13},{12,14},{13,15},{14,10},{15,... | collective-permute-start | bytes 3145736 | tf_op jit(solution)/shard_map/ppermute | solution.py:141
  25.5 54.2 %collective-permute-start.1 = (bf16[256,2048]{1,0:T(8,128)(2,1)S(1)}, bf16[256,2048]{1,0:T(8,128)(2,1)}, u32[]{:S(2)}, u32[]{:S(2)}) collective-permute-start(bf16[256,2048]{1,0:T(8,128)(2,1)S(1)} %constant_dynamic-update-slice_fusion.refs_0_.refs_1_), channel_id=1, source_target_pairs={{4,0},{5,1},{8,4},{9,5},{12,8},{13,9},{14,12},{15,13},{10,14},{11,... | collective-permute-start | bytes 3145736 | tf_op jit(solution)/shard_map/ppermute | solution.py:144
  25.6 67.9 %collective-permute-start.4 = (bf16[256,2048]{1,0:T(8,128)(2,1)S(1)}, bf16[256,2048]{1,0:T(8,128)(2,1)}, u32[]{:S(2)}, u32[]{:S(2)}) collective-permute-start(bf16[256,2048]{1,0:T(8,128)(2,1)S(1)} %constant_dynamic-update-slice_fusion.refs_0_.refs_1_), channel_id=1, source_target_pairs={{0,1},{1,0},{2,3},{3,2},{4,5},{5,4},{6,7},{7,6},{8,9},{9,8},{10,11... | collective-permute-start | bytes 3145736 | tf_op jit(solution)/shard_map/ppermute | solution.py:147
  79.8 34.6 %collective-permute-start.2 = (bf16[256,2048]{1,0:T(8,128)(2,1)}, bf16[256,2048]{1,0:T(8,128)(2,1)}, u32[]{:S(2)}, u32[]{:S(2)}) collective-permute-start(bf16[256,2048]{1,0:T(8,128)(2,1)} %collective-permute-done.refs_0_.refs_1_), channel_id=1, source_target_pairs={{0,4},{1,5},{4,8},{5,9},{8,12},{9,13},{12,14},{13,15},{14,10},{15,... | collective-permute-start | bytes 3145736 | tf_op jit(solution)/shard_map/ppermute | solution.py:141
  91.8 24.7 %collective-permute-start.3 = (bf16[256,2048]{1,0:T(8,128)(2,1)}, bf16[256,2048]{1,0:T(8,128)(2,1)}, u32[]{:S(2)}, u32[]{:S(2)}) collective-permute-start(bf16[256,2048]{1,0:T(8,128)(2,1)} %collective-permute-done.1.refs_2_.refs_3_), channel_id=1, source_target_pairs={{4,0},{5,1},{8,4},{9,5},{12,8},{13,9},{14,12},{15,13},{10,14},{11,... | collective-permute-start | bytes 3145736 | tf_op jit(solution)/shard_map/ppermute | solution.py:144
  91.8 25.9 %collective-permute-start.9 = (bf16[256,2048]{1,0:T(8,128)(2,1)}, bf16[256,2048]{1,0:T(8,128)(2,1)}, u32[]{:S(2)}, u32[]{:S(2)}) collective-permute-start(bf16[256,2048]{1,0:T(8,128)(2,1)} %collective-permute-done.refs_0_.refs_1_), channel_id=1, source_target_pairs={{0,1},{1,0},{2,3},{3,2},{4,5},{5,4},{6,7},{7,6},{8,9},{9,8},{10,11... | collective-permute-start | bytes 3145736 | tf_op jit(solution)/shard_map/ppermute | solution.py:147
  91.8 32.7 %collective-permute-start.10 = (bf16[256,2048]{1,0:T(8,128)(2,1)}, bf16[256,2048]{1,0:T(8,128)(2,1)}, u32[]{:S(2)}, u32[]{:S(2)}) collective-permute-start(bf16[256,2048]{1,0:T(8,128)(2,1)} %collective-permute-done.1.refs_2_.refs_3_), channel_id=1, source_target_pairs={{0,1},{1,0},{2,3},{3,2},{4,5},{5,4},{6,7},{7,6},{8,9},{9,8},{10,11... | collective-permute-start | bytes 3145736 | tf_op jit(solution)/shard_map/ppermute | solution.py:147
  116.6 16.6 %collective-permute-start.7 = (bf16[256,2048]{1,0:T(8,128)(2,1)}, bf16[256,2048]{1,0:T(8,128)(2,1)}, u32[]{:S(2)}, u32[]{:S(2)}) collective-permute-start(bf16[256,2048]{1,0:T(8,128)(2,1)} %collective-permute-done.2.refs_0_.refs_1_), channel_id=1, source_target_pairs={{0,1},{1,0},{2,3},{3,2},{4,5},{5,4},{6,7},{7,6},{8,9},{9,8},{10,11... | collective-permute-start | bytes 3145736 | tf_op jit(solution)/shard_map/ppermute | solution.py:147
  116.6 16.6 %collective-permute-start.8 = (bf16[256,2048]{1,0:T(8,128)(2,1)}, bf16[256,2048]{1,0:T(8,128)(2,1)}, u32[]{:S(2)}, u32[]{:S(2)}) collective-permute-start(bf16[256,2048]{1,0:T(8,128)(2,1)} %collective-permute-done.3.refs_2_.refs_3_), channel_id=1, source_target_pairs={{0,1},{1,0},{2,3},{3,2},{4,5},{5,4},{6,7},{7,6},{8,9},{9,8},{10,11... | collective-permute-start | bytes 3145736 | tf_op jit(solution)/shard_map/ppermute | solution.py:147
  117.1 25.3 %collective-permute-start.5 = (bf16[256,2048]{1,0:T(8,128)(2,1)}, bf16[256,2048]{1,0:T(8,128)(2,1)S(1)}, u32[]{:S(2)}, u32[]{:S(2)}) collective-permute-start(bf16[256,2048]{1,0:T(8,128)(2,1)} %collective-permute-done.2.refs_0_.refs_1_), channel_id=1, source_target_pairs={{0,4},{1,5},{4,8},{5,9},{8,12},{9,13},{12,14},{13,15},{14,10},{15,... | collective-permute-start | bytes 3145736 | tf_op jit(solution)/shard_map/ppermute | solution.py:141
  117.8 25.6 %collective-permute-start.6 = (bf16[256,2048]{1,0:T(8,128)(2,1)}, bf16[256,2048]{1,0:T(8,128)(2,1)}, u32[]{:S(2)}, u32[]{:S(2)}) collective-permute-start(bf16[256,2048]{1,0:T(8,128)(2,1)} %collective-permute-done.3.refs_2_.refs_3_), channel_id=1, source_target_pairs={{4,0},{5,1},{8,4},{9,5},{12,8},{13,9},{14,12},{15,13},{10,14},{11,... | collective-permute-start | bytes 3145736 | tf_op jit(solution)/shard_map/ppermute | solution.py:144
  163.6 63.7 %all-to-all-start.2 = ((bf16[16,96,768]{2,1,0:T(8,128)(2,1)}), bf16[16,96,768]{2,1,0:T(8,128)(2,1)S(1)}, u32[]{:S(2)}, u32[]{:S(2)}) async-start(bf16[16,96,768]{2,1,0:T(8,128)(2,1)} %bitcast.44), calls=%async_computation.2 | async-start | bytes 4718592 | tf_op jit(solution)/shard_map/all_to_all | solution.py:530
  183.5 43.7 %collective-permute-start.17 = (bf16[1024,512]{1,0:T(8,128)(2,1)}, bf16[1024,512]{1,0:T(8,128)(2,1)S(1)}, u32[]{:S(2)}, u32[]{:S(2)}) collective-permute-start(bf16[1024,512]{1,0:T(8,128)(2,1)} %get-tuple-element.180), channel_id=1, source_target_pairs={{0,16},{16,0},{1,17},{17,1},{2,18},{18,2},{3,19},{19,3},{4,20},{20... | collective-permute-start | bytes 3145736 | tf_op jit(solution)/shard_map/ppermute | solution.py:591
  203.4 45.2 %collective-permute-start.18 = (bf16[1024,768]{1,0:T(8,128)(2,1)}, bf16[1024,768]{1,0:T(8,128)(2,1)}, u32[]{:S(2)}, u32[]{:S(2)}) collective-permute-start(bf16[1024,768]{1,0:T(8,128)(2,1)} %get-tuple-element.184), channel_id=1, source_target_pairs={{0,16},{16,0},{1,17},{17,1},{2,18},{18,2},{3,19},{19,3},{4,20},{20... | collective-permute-start | bytes 4718600 | tf_op jit(solution)/shard_map/ppermute | solution.py:591
  247.0 54.4 %collective-permute-start.19 = (bf16[1024,768]{1,0:T(8,128)(2,1)}, bf16[1024,768]{1,0:T(8,128)(2,1)S(1)}, u32[]{:S(2)}, u32[]{:S(2)}) collective-permute-start(bf16[1024,768]{1,0:T(8,128)(2,1)} %get-tuple-element.195), channel_id=1, source_target_pairs={{0,16},{16,0},{1,17},{17,1},{2,18},{18,2},{3,19},{19,3},{4,20},{20... | collective-permute-start | bytes 4718600 | tf_op jit(solution)/shard_map/ppermute | solution.py:591
  266.7 53.9 %collective-permute-start.20 = (bf16[1024,768]{1,0:T(8,128)(2,1)}, bf16[1024,768]{1,0:T(8,128)(2,1)}, u32[]{:S(2)}, u32[]{:S(2)}) collective-permute-start(bf16[1024,768]{1,0:T(8,128)(2,1)} %get-tuple-element.202), channel_id=1, source_target_pairs={{0,16},{16,0},{1,17},{17,1},{2,18},{18,2},{3,19},{19,3},{4,20},{20... | collective-permute-start | bytes 4718600 | tf_op jit(solution)/shard_map/ppermute | solution.py:591
  301.4 94.3 %collective-permute-start.34 = (bf16[704,2048]{1,0:T(8,128)(2,1)}, bf16[704,2048]{1,0:T(8,128)(2,1)}, u32[]{:S(2)}, u32[]{:S(2)}) collective-permute-start(bf16[704,2048]{1,0:T(8,128)(2,1)} %constant_dynamic-slice_fusion), channel_id=1, source_target_pairs={{0,16},{16,0},{1,17},{17,1},{2,18},{18,2},{3,19},{19,3},{4,20},{20... | collective-permute-start | bytes 8650760 | tf_op jit(solution)/shard_map/ppermute | solution.py:613
  302.9 21.9 %collective-permute-start.24 = (bf16[256,2048]{1,0:T(8,128)(2,1)}, bf16[256,2048]{1,0:T(8,128)(2,1)S(1)}, u32[]{:S(2)}, u32[]{:S(2)}) collective-permute-start(bf16[256,2048]{1,0:T(8,128)(2,1)} %get-tuple-element.206), channel_id=1, source_target_pairs={{0,1},{1,0},{2,3},{3,2},{4,5},{5,4},{6,7},{7,6},{8,9},{9,8},{10,11... | collective-permute-start | bytes 3145736 | tf_op jit(solution)/shard_map/ppermute | solution.py:147
  302.9 17.8 %collective-permute-start.25 = (bf16[128,2048]{1,0:T(8,128)(2,1)}, bf16[128,2048]{1,0:T(8,128)(2,1)}, u32[]{:S(2)}, u32[]{:S(2)}) collective-permute-start(bf16[128,2048]{1,0:T(8,128)(2,1)} %get-tuple-element.205), channel_id=1, source_target_pairs={{0,1},{1,0},{2,3},{3,2},{4,5},{5,4},{6,7},{7,6},{8,9},{9,8},{10,11... | collective-permute-start | bytes 1572872 | tf_op jit(solution)/shard_map/ppermute | solution.py:147
  303.4 48.8 %collective-permute-start.23 = (bf16[256,2048]{1,0:T(8,128)(2,1)}, bf16[256,2048]{1,0:T(8,128)(2,1)S(1)}, u32[]{:S(2)}, u32[]{:S(2)}) collective-permute-start(bf16[256,2048]{1,0:T(8,128)(2,1)} %get-tuple-element.207), channel_id=1, source_target_pairs={{0,1},{1,0},{2,3},{3,2},{4,5},{5,4},{6,7},{7,6},{8,9},{9,8},{10,11... | collective-permute-start | bytes 3145736 | tf_op jit(solution)/shard_map/ppermute | solution.py:147
  336.9 15.2 %collective-permute-start.28 = (bf16[128,2048]{1,0:T(8,128)(2,1)}, bf16[128,2048]{1,0:T(8,128)(2,1)S(1)}, u32[]{:S(2)}, u32[]{:S(2)}) collective-permute-start(bf16[128,2048]{1,0:T(8,128)(2,1)} %get-tuple-element.227), channel_id=1, source_target_pairs={{0,4},{1,5},{4,8},{5,9},{8,12},{9,13},{12,14},{13,15},{14,10},{15,... | collective-permute-start | bytes 1572872 | tf_op jit(solution)/shard_map/ppermute | solution.py:141
  339.1 33.7 %collective-permute-start.22 = (bf16[256,2048]{1,0:T(8,128)(2,1)}, bf16[256,2048]{1,0:T(8,128)(2,1)S(1)}, u32[]{:S(2)}, u32[]{:S(2)}) collective-permute-start(bf16[256,2048]{1,0:T(8,128)(2,1)} %get-tuple-element.208), channel_id=1, source_target_pairs={{0,1},{1,0},{2,3},{3,2},{4,5},{5,4},{6,7},{7,6},{8,9},{9,8},{10,11... | collective-permute-start | bytes 3145736 | tf_op jit(solution)/shard_map/ppermute | solution.py:147
  359.1 28.3 %collective-permute-start.21 = (bf16[128,2048]{1,0:T(8,128)(2,1)S(1)}, bf16[128,2048]{1,0:T(8,128)(2,1)S(1)}, u32[]{:S(2)}, u32[]{:S(2)}) collective-permute-start(bf16[128,2048]{1,0:T(8,128)(2,1)S(1)} %copy-done.26), channel_id=1, source_target_pairs={{0,1},{1,0},{2,3},{3,2},{4,5},{5,4},{6,7},{7,6},{8,9},{9,8},{10,11... | collective-permute-start | bytes 1572872 | tf_op jit(solution)/shard_map/ppermute | solution.py:147
  (41 other events, 436.8 us)
